TPU v7x, 512 devices: a whole 4x4x16 slice. The times are simulated.
512 devices in a mesh: tensor: 8 (over y_lo, x), expert: 32 (over y_hi, z), dp: 2 (over core).
Axes of the slice: x: 4, y: 4 (y_hi: 2, y_lo: 2; y = y_hi * 2 + y_lo), z: 16, core: 2. Of those that a mesh axis runs over, the one named last changes fastest.
Arguments:
- patches: bfloat16 [64, 64, 4608], P(('dp', 'expert')), parts along dimension 0, may hold values from -700 to 700
- patch_gain: float32 [1152], replicated, may hold values from 0.5 to 1.5
- patch_bias: float32 [1152], replicated, may hold values from -3 to 3
- first_weight: bfloat16 [4608, 2304], P('expert', 'tensor'), may hold values from -0.09375 to 0.09375
- first_bias: float32 [2304], P('tensor'), may hold values from -3 to 3
- second_weight: bfloat16 [4096, 2304], P('expert', 'tensor'), may hold values from -0.125 to 0.125
- second_bias: float32 [4096], replicated, may hold values from -3 to 3
- image_units: int32 [64, 32], P(('dp', 'expert')), parts along dimension 0, may hold values from 1 to 2, as said below
- image_owner: int32 [64, 32], P(('dp', 'expert')), parts along dimension 0, may hold values from 0 to 31, as said below
- image_offset: int32 [64, 32], P(('dp', 'expert')), parts along dimension 0, may hold values from 0 to 127, as said below
- text_states: bfloat16 [64, 128, 4096], P(('dp', 'expert')), parts along dimension 0, may hold values from -700 to 700
- token_gain: float32 [4096], replicated, may hold values from 0.1 to 1.9
- expert_ids: int32 [64, 128, 8], P(('dp', 'expert')), parts along dimension 0, may hold values from 0 to 127, as said below
- route_weights: float32 [64, 128, 8], P(('dp', 'expert')), parts along dimension 0, may hold values from 0.1 to 1
- gate_weight: bfloat16 [32, 4096, 1024], P('expert', None, 'tensor'), may hold values from -0.09375 to 0.09375
- up_weight: bfloat16 [32, 4096, 1024], P('expert', None, 'tensor'), may hold values from -0.09375 to 0.09375
- down_weight: bfloat16 [32, 1024, 4096], P('expert', None, 'tensor'), may hold values from -0.1875 to 0.1875
Outputs:
- mixed: bfloat16 [64, 128, 4096], P(('dp', 'expert'), None, 'tensor'), parts along dimension 0
There are 2 independent parts, one for each index of `dp`. A program takes and returns all parts, laid end to end along the dimension named above; an argument that names none is the same for every part. Nothing has to cross between parts.
Inputs may be any that keep to these rules, and one draw needn't show every extreme that they name: `image_units`: A group's images stand one after another from its first unit. In every draw one owner receives 32 images of 2 tokens each, and one group's images fill all 64 units. `image_owner`: image k of group g goes to owner (g + s_k) mod 32, with 32 different shifts s_k, so a group sends exactly one image to each owner and every owner receives 32 images. `image_offset`: image k lies within positions k * 4 to (k + 1) * 4 - 1 of its owner's sequence, so the images of one owner never share a position. `expert_ids`: each token names 8 different experts; those below 32 are in flight. No expert is named by more than 16 tokens of one owner's sequence, and one expert in flight is named by exactly 16 tokens of every owner's sequence.
All inputs are finite; a program needn't handle non-finite values.
Results may differ from a plain program's by a relative error of at most 0.0082.
Values may be sent and summed in bfloat16 or wider, within the bound.
A program may use at most 64 MiB of HBM per device.

v0:
```python
import jax
import jax.numpy as jnp
from jax import lax
from jax.sharding import PartitionSpec as P


def normalize_patches(patches, patch_gain, patch_bias):
    values = patches[0].astype(jnp.float32)
    unit_count, row_width = values.shape
    vision = patch_gain.shape[0]
    pieces = values.reshape(unit_count, row_width // vision, vision)
    center = pieces - jnp.mean(pieces, axis=2, keepdims=True)
    variance = jnp.mean(center * center, axis=2, keepdims=True)
    scaled = center * lax.rsqrt(variance + 1e-06) * patch_gain + patch_bias
    return scaled.astype(jnp.bfloat16).reshape(unit_count, row_width)


def run_experts(arrivals, gate_matrix, up_matrix, down_matrix):
    gate_proj = jnp.einsum("snd,dh->snh", arrivals, gate_matrix, preferred_element_type=jnp.float32)
    up_proj = jnp.einsum("snd,dh->snh", arrivals, up_matrix, preferred_element_type=jnp.float32)
    activation = (jax.nn.silu(gate_proj) * up_proj).astype(jnp.bfloat16)
    all_hidden = lax.all_gather(activation, "tensor", axis=2, tiled=True)
    produced = jnp.einsum(
        "snh,hd->snd", all_hidden, down_matrix, preferred_element_type=jnp.float32
    ).astype(jnp.bfloat16)
    return lax.all_to_all(produced, "expert", split_axis=0, concat_axis=0, tiled=True)


def body(
    patches,
    patch_gain,
    patch_bias,
    first_weight,
    first_bias,
    second_weight,
    second_bias,
    image_units,
    image_owner,
    image_offset,
    text_states,
    token_gain,
    expert_ids,
    route_weights,
    gate_weight,
    up_weight,
    down_weight,
):
    groups = lax.axis_size("expert")
    unit_rows = normalize_patches(patches, patch_gain, patch_bias)
    unit_count = unit_rows.shape[0]
    first_full, second_full = (
        lax.all_gather(first_weight, "expert", axis=0, tiled=True),
        lax.all_gather(second_weight, "expert", axis=0, tiled=True),
    )
    first_out = jnp.dot(unit_rows, first_full, preferred_element_type=jnp.float32)
    merger_hidden = jax.nn.gelu(first_out + first_bias, approximate=False).astype(jnp.bfloat16)
    partial_sum = lax.dot_general(
        merger_hidden, second_full, (((1,), (1,)), ((), ())), preferred_element_type=jnp.float32
    )
    model_width = partial_sum.shape[1]
    summed = lax.psum(partial_sum, "tensor")
    embedded = (summed + second_bias).astype(jnp.bfloat16)
    base_states = text_states[0]
    counts = image_units[0]
    owners = image_owner[0]
    offsets = image_offset[0]
    starts = jnp.cumsum(counts) - counts
    images = counts.shape[0]
    longest = unit_count // images
    seq_len = text_states.shape[1]
    slot_index = jnp.arange(longest, dtype=jnp.int32)[None, :]
    dest_owner = jnp.arange(groups, dtype=jnp.int32)[:, None]
    match_table = (owners[None, :] == dest_owner).astype(jnp.int32)
    dest_start = jnp.sum(match_table * starts[None, :], axis=1)[:, None]
    dest_count = jnp.sum(match_table * counts[None, :], axis=1)[:, None]
    dest_offset = jnp.sum(match_table * offsets[None, :], axis=1)[:, None]
    hit_mask = slot_index < dest_count
    source = jnp.where(hit_mask, dest_start + slot_index, 0)
    target_pos = jnp.where(hit_mask, dest_offset + slot_index, seq_len)
    outgoing = jnp.take(embedded, source.reshape(-1), axis=0).reshape(
        groups, longest, embedded.shape[1]
    )
    arrived, positions = (
        lax.all_to_all(outgoing, "expert", split_axis=0, concat_axis=0, tiled=True),
        lax.all_to_all(target_pos, "expert", split_axis=0, concat_axis=0, tiled=True),
    )
    states = base_states.at[positions.reshape(-1)].set(
        arrived.reshape(groups * longest, arrived.shape[2]), mode="drop"
    )
    widened = states.astype(jnp.float32)
    squares = jnp.sum(widened * widened, axis=1, keepdims=True)
    inverse = lax.rsqrt(squares / model_width + 1e-06)
    normed = (widened * inverse * token_gain).astype(jnp.bfloat16)
    routes = expert_ids[0]
    route_share = route_weights[0]
    pick_count = routes.shape[1]
    capacity = 2 * seq_len * pick_count // (4 * groups)
    expert_row = jnp.arange(groups, dtype=jnp.int32)
    member = jnp.any(routes[:, :, None] == expert_row, axis=1).astype(jnp.int32)
    rank_table = jnp.cumsum(member, axis=0) - member
    in_flight = routes < groups
    safe_ids = jnp.where(in_flight, routes, 0)
    slot_rank = jnp.take_along_axis(rank_table, safe_ids, axis=1)
    flat_slot = jnp.where(in_flight, safe_ids * capacity + slot_rank, groups * capacity)
    copies = jnp.broadcast_to(normed[:, None, :], (seq_len, pick_count, model_width)).reshape(
        seq_len * pick_count, model_width
    )
    dispatched = (
        jnp.zeros((groups * capacity, model_width), jnp.bfloat16)
        .at[flat_slot.reshape(-1)]
        .set(copies, mode="drop")
    )
    dispatched = dispatched.reshape(groups, capacity, model_width)
    returned = run_experts(
        lax.all_to_all(dispatched, "expert", split_axis=0, concat_axis=0, tiled=True),
        gate_weight[0],
        up_weight[0],
        down_weight[0],
    )
    out_width = returned.shape[2]
    lookup = jnp.where(in_flight, safe_ids * capacity + slot_rank, 0).reshape(-1)
    gathered = jnp.take(returned.reshape(groups * capacity, out_width), lookup, axis=0).reshape(
        seq_len, pick_count, out_width
    )
    weighted = jnp.where(in_flight, route_share, 0.0)
    mixed_out = jnp.sum(gathered.astype(jnp.float32) * weighted[:, :, None], axis=1)
    return mixed_out.astype(jnp.bfloat16)[None]


def solution(mesh):
    in_specs = (
        P(("dp", "expert"), None, None),
        P(),
        P(),
        P("expert", "tensor"),
        P("tensor"),
        P("expert", "tensor"),
        P(),
        P(("dp", "expert"), None),
        P(("dp", "expert"), None),
        P(("dp", "expert"), None),
        P(("dp", "expert"), None, None),
        P(),
        P(("dp", "expert"), None, None),
        P(("dp", "expert"), None, None),
        P("expert", None, "tensor"),
        P("expert", None, "tensor"),
        P("expert", None, "tensor"),
    )
    out_specs = P(("dp", "expert"), None, "tensor")
    return jax.shard_map(body, mesh=mesh, in_specs=in_specs, out_specs=out_specs, check_vma=False)
```

profile of v0, /device:TPU:32, one launch (start us, length us, event | category | flops | bytes accessed | tf_op | source)
XLA Modules:
  0.0 766.9 jit_solution(14707322154439758728)
XLA Ops:
  6.5 0.7 all-gather.6.cloned.1.call-update
  10.5 152.2 %all-gather.6.cloned.1.call-done = bf16[4096,288]{0,1:T(8,128)(2,1)} async-done(((bf16[128,288]{0,1:T(8,128)(2,1)}), bf16[4096,288]{0,1:T(8,128)(2,1)}) %all-gather.6.cloned.1.call-update) | async-done | bytes 2359312 | tf_op jit(solution)/shard_map/all_gather | solution.py:53
  162.8 157.5 %all-gather.4.cloned.1.call-done = bf16[4608,288]{1,0:T(8,128)(2,1)} async-done(((bf16[144,288]{1,0:T(8,128)(2,1)}), bf16[4608,288]{1,0:T(8,128)(2,1)}) %all-gather.4.cloned.1.call-update) | async-done | bytes 2654224 | tf_op jit(solution)/shard_map/all_gather | solution.py:52
  320.3 5.7 fusion.34
  326.1 0.8 compare_select_fusion.2
  326.9 7.8 %all-to-all-start = ((s32[32,1,2]{2,1,0:T(1,128)}), s32[32,1,2]{2,1,0:T(1,128)S(1)}, u32[]{:S(2)}, u32[]{:S(2)}) async-start(s32[32,1,2]{2,1,0:T(1,128)} %compare_select_fusion.2), calls=%async_computation | async-start | bytes 32768 | tf_op jit(solution)/shard_map/all_to_all | solution.py:85
  335.0 78.0 %all-reduce.2.cloned.1.call-done = f32[64,4096]{1,0:T(8,128)} async-done(((f32[64,4096]{1,0:T(8,128)}), f32[64,4096]{1,0:T(8,128)}) %all-reduce.2.cloned.1.call-update) | async-done | bytes 1048592 | tf_op jit(solution)/shard_map/psum | solution.py:61
  413.0 1.3 add_convert_fusion
  414.3 0.9 gather_fusion
  415.6 1.4 broadcast_select_fusion
  416.9 15.0 %all-to-all-start.1 = ((bf16[32,2,4096]{2,1,0:T(2,128)(2,1)}), bf16[32,2,4096]{2,1,0:T(2,128)(2,1)S(1)}, u32[]{:S(2)}, u32[]{:S(2)}) async-start(bf16[32,2,4096]{2,1,0:T(2,128)(2,1)} %broadcast_select_fusion), calls=%async_computation.1 | async-start | bytes 1048576 | tf_op jit(solution)/shard_map/all_to_all | solution.py:84
  432.7 7.1 gather_fusion.2
  441.2 19.9 %all-to-all-done.1 = bf16[32,2,4096]{2,1,0:T(2,128)(2,1)S(1)} async-done(((bf16[32,2,4096]{2,1,0:T(2,128)(2,1)}), bf16[32,2,4096]{2,1,0:T(2,128)(2,1)S(1)}, u32[]{:S(2)}, u32[]{:S(2)}) %all-to-all-start.1) | async-done | bytes 524320 | tf_op jit(solution)/shard_map/all_to_all | solution.py:84
  461.3 2.1 scatter_fusion
  464.0 13.7 %scatter_custom_fusion.1 = bf16[512,4096]{1,0:T(8,128)(2,1)} fusion(s32[1024]{0:T(1024)S(1)} %bitcast.87, bf16[128,4096]{1,0:T(8,128)(2,1)S(1)} %fusion.5, bf16[]{:T(256)} %constant.30.clone.1), kind=kCustom, calls=%fused_computation.5 | custom fusion | bytes 5242882 | tf_op jit(solution)/shard_map/scatter | solution.py:111
  477.7 191.1 %all_to_all.21 = bf16[32,16,4096]{2,1,0:T(8,128)(2,1)S(1)} all-to-all(bf16[32,16,4096]{2,1,0:T(8,128)(2,1)} %bitcast.79), channel_id=1, replica_groups=mesh['tensor'=8,'expert'=32,'dp'=2] {'expert'}, dimensions={0} | all-to-all | bytes 8388608 | tf_op jit(solution)/shard_map/all_to_all | solution.py:115
  668.8 1.3 fusion.14
  670.0 1.9 fusion.11
  672.0 34.8 %all-gather.8.cloned.1.call-done = bf16[32,16,1024]{2,1,0:T(8,128)(2,1)} async-done(((bf16[32,16,128]{2,1,0:T(8,128)(2,1)}), bf16[32,16,1024]{2,1,0:T(8,128)(2,1)}) %all-gather.8.cloned.1.call-update) | async-done | bytes 1048592 | tf_op jit(solution)/shard_map/all_gather | solution.py:22
  706.8 2.8 convolution_convert_fusion
  709.5 15.3 %all-to-all-start.3 = ((bf16[32,16,512]{2,1,0:T(8,128)(2,1)}), bf16[32,16,512]{2,1,0:T(8,128)(2,1)S(1)}, u32[]{:S(2)}, u32[]{:S(2)}) async-start(bf16[32,16,512]{2,1,0:T(8,128)(2,1)} %convolution_convert_fusion), calls=%async_computation.3 | async-start | bytes 1048576 | tf_op jit(solution)/shard_map/all_to_all | solution.py:26
  725.2 29.8 %all-to-all-done.3 = bf16[32,16,512]{2,1,0:T(8,128)(2,1)S(1)} async-done(((bf16[32,16,512]{2,1,0:T(8,128)(2,1)}), bf16[32,16,512]{2,1,0:T(8,128)(2,1)S(1)}, u32[]{:S(2)}, u32[]{:S(2)}) %all-to-all-start.3) | async-done | bytes 524320 | tf_op jit(solution)/shard_map/all_to_all | solution.py:26
  754.9 4.0 gather_fusion.1
  758.9 1.4 multiply_reduce_fusion
  (85 shorter events, 7.1 us)
Async XLA Ops:
  6.5 700.2 %copy-start = (bf16[1,1024,512]{2,1,0:T(8,128)(2,1)S(1)}, bf16[1,1024,512]{2,1,0:T(8,128)(2,1)}, u32[]{:S(2)}) copy-start(bf16[1,1024,512]{2,1,0:T(8,128)(2,1)} %param.33) | copy-start | bytes 3145732
  6.5 1.5 copy-start.2
  6.5 156.2 %all-gather.6.cloned.1.call-start = ((), (), s32[]{:S(2)}) async-start(), calls=%async_computation.5 | async-start | bytes 2433024 | tf_op jit(solution)/shard_map/all_gather | solution.py:53
  7.3 313.0 %all-gather.4.cloned.1.call-start = ((), (), s32[]{:S(2)}) async-start(), calls=%async_computation.4 | async-start | bytes 3649536 | tf_op jit(solution)/shard_map/all_gather | solution.py:52
  8.0 405.0 %all-reduce.2.cloned.1.call-start = ((), (), s32[]{:S(2)}) async-start(), calls=%async_computation.6 | async-start | bytes 2097152 | tf_op jit(solution)/shard_map/psum | solution.py:61
  9.5 0.7 copy-start.7
  9.6 0.7 copy-start.8
  9.6 0.7 copy-start.11
  9.6 310.7 %copy-start.10 = (f32[288]{0:T(512)S(1)}, f32[288]{0:T(512)}, u32[]{:S(2)}) copy-start(f32[288]{0:T(512)} %param.21) | copy-start | bytes 3460
  320.3 5.7 copy-start.12
  320.3 5.7 copy-start.13
  320.3 92.8 %copy-start.5 = (f32[4096]{0:T(1024)S(1)}, f32[4096]{0:T(1024)}, u32[]{:S(2)}) copy-start(f32[4096]{0:T(1024)} %param.23) | copy-start | bytes 49156
  326.9 90.0 %all-to-all-start = ((s32[32,1,2]{2,1,0:T(1,128)}), s32[32,1,2]{2,1,0:T(1,128)S(1)}, u32[]{:S(2)}, u32[]{:S(2)}) async-start(s32[32,1,2]{2,1,0:T(1,128)} %compare_select_fusion.2), calls=%async_computation | async-start | bytes 32768 | tf_op jit(solution)/shard_map/all_to_all | solution.py:85
  415.2 16.7 %copy-start.4 = (s32[1,128,8]{1,2,0:T(8,128)S(1)}, s32[1,128,8]{1,2,0:T(8,128)}, u32[]{:S(2)}) copy-start(s32[1,128,8]{1,2,0:T(8,128)} %param.29) | copy-start | bytes 12292
  416.9 44.1 %all-to-all-start.1 = ((bf16[32,2,4096]{2,1,0:T(2,128)(2,1)}), bf16[32,2,4096]{2,1,0:T(2,128)(2,1)S(1)}, u32[]{:S(2)}, u32[]{:S(2)}) async-start(bf16[32,2,4096]{2,1,0:T(2,128)(2,1)} %broadcast_select_fusion), calls=%async_computation.1 | async-start | bytes 1048576 | tf_op jit(solution)/shard_map/all_to_all | solution.py:84
  431.9 274.9 %all-gather.8.cloned.1.call-start = ((), (), s32[]{:S(2)}) async-start(), calls=%async_computation.7 | async-start | bytes 1179648 | tf_op jit(solution)/shard_map/all_gather | solution.py:22
  439.8 21.4 %copy-start.1 = (bf16[1,128,4096]{2,1,0:T(8,128)(2,1)S(1)}, bf16[1,128,4096]{2,1,0:T(8,128)(2,1)}, u32[]{:S(2)}) copy-start(bf16[1,128,4096]{2,1,0:T(8,128)(2,1)} %param.27) | copy-start | bytes 3145732
  461.2 2.4 copy-start.6
  477.7 191.1 %copy-start.3 = (bf16[1,4096,128]{2,1,0:T(8,128)(2,1)S(1)}, bf16[1,4096,128]{2,1,0:T(8,128)(2,1)}, u32[]{:S(2)}) copy-start(bf16[1,4096,128]{2,1,0:T(8,128)(2,1)} %param.31) | copy-start | bytes 3145732
  668.8 1.3 copy-start.14
  672.0 53.0 %copy-start.9 = (f32[1,128,8]{1,2,0:T(8,128)S(1)}, f32[1,128,8]{1,2,0:T(8,128)}, u32[]{:S(2)}) copy-start(f32[1,128,8]{1,2,0:T(8,128)} %param.30) | copy-start | bytes 12292
  709.5 45.4 %all-to-all-start.3 = ((bf16[32,16,512]{2,1,0:T(8,128)(2,1)}), bf16[32,16,512]{2,1,0:T(8,128)(2,1)S(1)}, u32[]{:S(2)}, u32[]{:S(2)}) async-start(bf16[32,16,512]{2,1,0:T(8,128)(2,1)} %convolution_convert_fusion), calls=%async_computation.3 | async-start | bytes 1048576 | tf_op jit(solution)/shard_map/all_to_all | solution.py:26
Sparse Core Ops, SparseCore 0:
  10.3 152.4 all-gather.5
  165.9 154.3 all-gather.3
  326.1 86.9 all-reduce.1
  672.1 34.6 all-gather.7
where the time goes:
time: 768 us; the launch traced here: 767 us
  waiting for transfers between devices  474 us (62%)
  blocking collectives  191 us (25%)
  starting transfers between devices  38.3 us (5%)
  local copies, waits for them, and re-layouts  31.1 us (4%)
  between operations  13.5 us (2%)
  matrix products  11.6 us (2%)
  other arithmetic  7.69 us (1%)
    all_to_all x1, blocking collectives, body(): lax.all_to_all(dispatched, 'expert', split_axis=0, concat_axis=0, tiled=T...  191 us
    all_gather x1, waiting for transfers between devices, body(): lax.all_gather(first_weight, 'expert', axis=0, tiled=True)  157 us
    all_gather x1, waiting for transfers between devices, body(): lax.all_gather(second_weight, 'expert', axis=0, tiled=True)  152 us
    psum x1, waiting for transfers between devices, body(): summed = lax.psum(partial_sum, 'tensor')  78 us
    all_gather x1, waiting for transfers between devices, run_experts(): all_hidden = lax.all_gather(activation, 'tensor', axis=2, tiled=True)  34.8 us
    all_to_all x1, waiting for transfers between devices, run_experts(): lax.all_to_all(produced, 'expert', split_axis=0, concat_axis=0, tiled=True)  29.8 us
    all_to_all x1, waiting for transfers between devices, body(): lax.all_to_all(outgoing, 'expert', split_axis=0, concat_axis=0, tiled=True)  19.9 us
  transfers between devices with their start and end apart: 7, of which 6 were waited for; matrix products, arithmetic and copies ran while one was open for 2% of the time, Pallas kernels for 0%

commit v1 on v0

v1 whole, which is shorter than its diff:
```python
import jax
import jax.numpy as jnp
from jax import lax
from jax.experimental import pallas as pl
from jax.experimental.pallas import tpu as pltpu
from jax.sharding import PartitionSpec as P

BF = jnp.bfloat16
F32 = jnp.float32
I32 = jnp.int32
MESH = pl.DeviceIdType.MESH

PLANES = 16
CHUNKS = 4
PER = PLANES // CHUNKS
ROWS = PER * 32


def offset_of(place):
    if place == 0:
        return 0
    return (place + 1) // 2 if place % 2 else PLANES - place // 2


def nn(a, b):
    return jnp.dot(a, b, preferred_element_type=F32)


def nt(a, b):
    return lax.dot_general(a, b, (((1,), (1,)), ((), ())), preferred_element_type=F32)


def tn(a, b):
    return lax.dot_general(a, b, (((0,), (0,)), ((), ())), preferred_element_type=F32)


def wait(ref, sem):
    pltpu.make_async_copy(ref, ref, sem).wait()


def kernel(
    patches, pgain, pbias, w1, b1, w2, b2, units, owners, offsets, text, tgain,
    ids, shares, gate, up, down,
    out,
    g1, g2, pv, xn, b1p, hid, p1s, p1r, p2s, p2r, sel_own, sel_far, info_s, info_r,
    img_s, img_r, tx, rt, wt, pick, st, xs, xr, xk, wgu, dw, gx, ps, pr, ss_s, ss_r,
    act_s, act_r, ob, rb,
    s_w, r_w, s_c, r_c, l_sem, s_gu, r_gu, s_one, r_one, s_info, r_info, s_p2, r_p2,
    s_img, r_img, s_disp, r_disp, s_ag, r_ag, s_rs, r_rs, s_ss, r_ss, s_act, r_act,
    s_ret, r_ret,
):
    e = lax.axis_index("expert")
    t = lax.axis_index("tensor")
    core = lax.axis_index("dp")
    yh, z = e // 16, e % 16
    yl, x = t // 4, t % 4
    y = 2 * yh + yl
    far = (1 - yh) * 16 + z
    col = yh * 2048 + x * 512 + yl * 256
    far_col = (1 - yh) * 2048 + x * 512 + yl * 256

    def send(src, dst, ssem, rsem, **dev):
        copy = pltpu.make_async_remote_copy(
            src_ref=src, dst_ref=dst, send_sem=ssem, recv_sem=rsem,
            device_id=dev, device_id_type=MESH,
        )
        copy.start()
        return copy

    local = [
        (patches.at[0, :, pl.ds(pl.multiple_of(2304 * yh, 128), 2304)], pv.at[yh]),
        (text.at[0, :, pl.ds(pl.multiple_of(col, 128), 256)], tx.at[yh]),
        (down.at[0], dw),
    ]
    for h in range(2):
        rows = pl.ds(pl.multiple_of(2048 * h + 512 * x, 512), 512)
        local.append((gate.at[0, rows, :], wgu.at[x, pl.ds(512 * h, 512), pl.ds(0, 128)]))
        local.append((up.at[0, rows, :], wgu.at[x, pl.ds(512 * h, 512), pl.ds(128, 128)]))
    local = [pltpu.make_async_copy(a, b, l_sem.at[i]) for i, (a, b) in enumerate(local)]
    for copy in local:
        copy.start()

    barrier = pltpu.get_barrier_semaphore()

    def greet(**dev):
        pl.semaphore_signal(barrier, inc=1, device_id=dev, device_id_type=MESH)

    for i in range(1, 32):
        greet(expert=lax.rem(e + i, 32))
    for i in range(1, 8):
        greet(tensor=lax.rem(t + i, 8))
    greet(dp=1 - core)
    greet(expert=far, tensor=lax.rem(t + 4, 8))

    g1[z, :, 256:] = jnp.zeros((144, 128), BF)
    g2[z, :, 256:] = jnp.zeros((128, 128), BF)
    g1[z, :, :288] = w1[...]
    g2[z, :, :288] = w2[...]
    b1p[...] = jnp.zeros((1, 384), F32)
    b1p[:, :288] = b1[...]

    pl.semaphore_wait(barrier, 40)

    step_z = 1 - 2 * core
    nxt = yh * 16 + lax.rem(z + step_z + 16, 16)
    sends = []
    gathered = (g1, g2)
    for w, g in enumerate(gathered):
        sends.append(send(g.at[z], g.at[z], s_w.at[w, 0], r_w.at[w, 0], expert=nxt))
    far_half = pl.ds(pl.multiple_of(2304 * (1 - yh), 128), 2304)
    sends.append(send(patches.at[0, :, far_half], pv.at[yh], s_one.at[0], r_one.at[0], expert=far))
    far_cols = pl.ds(pl.multiple_of(far_col, 128), 256)
    sends.append(send(text.at[0, :, far_cols], tx.at[yh], s_one.at[1], r_one.at[1], expert=far))
    for i in range(1, 4):
        xx = lax.rem(x + i, 4)
        for h in range(2):
            rows = pl.ds(pl.multiple_of(2048 * h + 512 * xx, 512), 512)
            for k, source in enumerate((gate, up)):
                send(
                    source.at[0, rows, :],
                    wgu.at[x, pl.ds(512 * h, 512), pl.ds(128 * k, 128)],
                    s_gu, r_gu, tensor=yl * 4 + xx,
                )

    def iota(shape, dim):
        return lax.broadcasted_iota(I32, shape, dim)

    def route():
        lane = iota((128, 128), 1)
        place = lane >> 1
        dist = jnp.where((place & 1) == 1, (place + 1) >> 1, (16 - (place >> 1)) & 15)
        expert = jnp.where(lane < 32, (lane & 1) * 16 + ((z + dist) & 15), -1)
        member = jnp.zeros((128, 128), F32)
        share = jnp.zeros((128, 128), F32)
        for k in range(8):
            named = ids[:, k : k + 1] == expert
            member = jnp.where(named, 1.0, member)
            share = share + jnp.where(named, shares[:, k : k + 1], 0.0)
        before = (iota((128, 128), 1) < iota((128, 128), 0)).astype(F32).astype(BF)
        rank = nn(before, member.astype(BF))
        rt[yh] = jnp.where(member > 0.5, rank, -1.0).T[:32].astype(BF)
        wt[...] = share.T[:32]
        sends.append(send(rt.at[yh], rt.at[yh], s_one.at[2], r_one.at[2], expert=far))

    def images():
        unit_row = units[...].astype(F32)
        first = (iota((32, 32), 0) < iota((32, 32), 1)).astype(F32).astype(BF)
        starts = nn(jnp.broadcast_to(unit_row, (8, 32)).astype(BF), first)[:1]
        slot = iota((128, 32), 0)
        owner = ((slot >> 1) & 1) * 16 + ((z + (slot >> 3)) & 15)
        match = (owners[...] == owner) & (((slot >> 2) & 1) == yh)

        def pick_out(row):
            return jnp.sum(jnp.where(match, row, 0.0), axis=1, keepdims=True)

        start, count = pick_out(starts), pick_out(unit_row)
        offset = pick_out(offsets[...].astype(F32))
        column = iota((128, 1), 0)
        turn = (column & 1).astype(F32)
        valid = turn < count
        base = (yh * 64).astype(F32)
        source = jnp.where(valid, base + start + turn, -1.0)
        position = jnp.where(valid, ((column >> 1) & 1).astype(F32) * 128.0 + offset + turn, -1.0)
        sel_own[...] = (iota((128, 128), 1).astype(F32) == source).astype(F32).astype(BF)
        info_s[...] = jnp.broadcast_to(position, (128, 128)).reshape(16, 8, 128)
        info_r[yh * 16] = info_s[0]
        sends.append(send(sel_own, sel_far, s_one.at[3], r_one.at[3], expert=far))
        for d in range(16):
            zz = lax.rem(z + d, 16)
            dst = info_r.at[yh * 16 + d]
            send(info_s.at[d], dst, s_info, r_info, expert=(1 - yh) * 16 + zz)
            if d > 0:
                send(info_s.at[d], dst, s_info, r_info, expert=yh * 16 + zz)

    def norm_patches(own):
        g = yh if own else 1 - yh
        if own:
            local[0].wait()
        else:
            wait(pv.at[g], r_one.at[0])
        for p in range(2):
            part = pl.ds(1152 * p, 1152)
            v = pv[g, :, part].astype(F32)
            center = v - jnp.mean(v, axis=1, keepdims=True)
            variance = jnp.mean(center * center, axis=1, keepdims=True)
            scaled = center * lax.rsqrt(variance + 1e-06) * pgain[...] + pbias[...]
            xn[g, :, part] = scaled.astype(BF)

    def selections():
        wait(rt.at[1 - yh], r_one.at[2])
        for oy in range(2):
            ranks = rt[oy].astype(F32).reshape(32, 1, 128)
            slots = iota((32, 16, 128), 1).astype(F32)
            pick[oy] = (ranks == slots).astype(F32).reshape(512, 128).astype(BF)

    jobs = {
        0: [route, images],
        1: [lambda: norm_patches(True)],
        2: [lambda: norm_patches(False)],
        3: [selections],
    }
    for s in range(8):
        origin = lax.rem(z - step_z * (s + 1) + 32, 16)
        for w, g in enumerate(gathered):
            wait(g.at[origin], r_w.at[w, s])
            if s < 7:
                block = g.at[origin]
                sends.append(send(block, block, s_w.at[w, s + 1], r_w.at[w, s + 1], expert=nxt))
                sends.append(send(block, block, s_c.at[w, s], r_c.at[w, s], dp=1 - core))
        for job in jobs.get(s, ()):
            job()

    def other_core(w):
        for s in range(7):
            origin = lax.rem(z + step_z * (s + 1) + 32, 16)
            wait(gathered[w].at[origin], r_c.at[w, s])

    other_core(0)
    part1 = nn(xn[...].reshape(128, 2304), g1[...].reshape(2304, 384))
    p1s[...] = part1.astype(BF)
    sends.append(send(p1s, p1r, s_one.at[4], r_one.at[4], expert=far))
    other_core(1)
    wait(p1r, r_one.at[4])
    v = part1 + p1r[...].astype(F32) + b1p[...]
    hid[...] = (0.5 * v * (1.0 + lax.erf(v * (0.5**0.5)))).astype(BF)

    def second(tt):
        k = 2 * lax.rem(tt, 4) + tt // 4
        return nt(hid[...], g2[pl.ds(2 * k, 2)].reshape(256, 384))

    for i in range(1, 8):
        tt = lax.rem(t + i, 8)
        p2s[i - 1] = second(tt).astype(BF)
        send(p2s.at[i - 1], p2r.at[i - 1], s_p2, r_p2, tensor=tt)
    total = second(t) + b2[:, pl.ds(pl.multiple_of(col, 128), 256)]
    wait(info_r.at[pl.ds(0, 31)], r_info)
    wait(sel_far, r_one.at[3])
    chosen = sel_own[...] + sel_far[...]
    wait(p2r.at[pl.ds(0, 7)], r_p2)
    for i in range(7):
        total = total + p2r[i].astype(F32)
    emb = total.astype(BF)

    rows = nn(chosen, emb).reshape(16, 8, 256)
    img_s[...] = jnp.concatenate([rows[:, :, :128], rows[:, :, 128:]], axis=1).astype(BF)
    img_r[0] = img_s[0]
    for d in range(1, 16):
        send(img_s.at[d], img_r.at[d], s_img, r_img, expert=yh * 16 + lax.rem(z + d, 16))

    local[1].wait()
    wait(tx.at[1 - yh], r_one.at[1])
    position = jnp.maximum(info_r[pl.ds(0, 16)], info_r[pl.ds(16, 16)])
    blank = jnp.zeros((16, 8, 128), F32)
    placed = []
    for oy in range(2):
        hit = (position == (iota((16, 8, 128), 2) + oy * 128).astype(F32)).astype(F32)
        low = jnp.concatenate([hit, blank], axis=1).reshape(256, 128).astype(BF)
        high = jnp.concatenate([blank, hit], axis=1).reshape(256, 128).astype(BF)
        covered = tn(low, jnp.ones((256, 128), BF)) > 0.5
        placed.append((low, high, covered))
    wait(img_r.at[pl.ds(0, 15)], r_img)
    arrived = img_r[...].reshape(256, 128)
    for oy in range(2):
        low, high, covered = placed[oy]
        for half, hits in enumerate((low, high)):
            part = pl.ds(128 * half, 128)
            base = tx[oy, :, part].astype(F32)
            st[oy, :, part] = jnp.where(covered, tn(hits, arrived), base).astype(BF)

    for oy in range(2):
        xs[:, :, 16 * oy : 16 * oy + 16, :] = nn(pick[oy], st[oy]).astype(BF).reshape(16, 2, 16, 256)
    for p in range(1, 16):
        send(xs.at[p], xr.at[p], s_disp, r_disp.at[p], expert=yh * 16 + lax.rem(z + offset_of(p), 16))

    def forward(c):
        for p in range(PER * c, PER * c + PER):
            if p > 0:
                wait(xr.at[p], r_disp.at[p])
            block = xs.at[p] if p == 0 else xr.at[p]
            xk[p, y] = block[yh]
            dst = xk.at[p, y]
            send(block.at[yh], dst, s_ag, r_ag.at[c], tensor=lax.rem(t + 4, 8))
            send(block.at[1 - yh], dst, s_ag, r_ag.at[c], expert=far)
            send(block.at[1 - yh], dst, s_ag, r_ag.at[c], expert=far, tensor=lax.rem(t + 4, 8))

    def project(c):
        wait(xk.at[pl.ds(PER * c, 3)], r_ag.at[c])
        if c == 0:
            for copy in local[3:]:
                copy.wait()
            wait(wgu.at[pl.ds(0, 3)], r_gu)
        squares = jnp.zeros((8, ROWS), F32)
        ones = jnp.ones((8, 256), BF)
        for yy in range(4):
            v = xk[PER * c : PER * c + PER, yy].reshape(ROWS, 256).astype(F32)
            start = 2048 * (yy // 2) + 256 * (yy % 2) + 512 * x
            gain = tgain[:, pl.ds(pl.multiple_of(start, 128), 256)]
            gx[:, 256 * yy : 256 * yy + 256] = (v * gain).astype(BF)
            square = v * v
            high = square.astype(BF)
            low = (square - high.astype(F32)).astype(BF)
            squares = squares + nt(ones, high) + nt(ones, low)
        ss_s[c] = squares
        for i in range(1, 4):
            xx = lax.rem(x + i, 4)
            send(ss_s.at[c], ss_r.at[c, i - 1], s_ss, r_ss.at[c], tensor=yl * 4 + xx)
            ps[c, i] = nn(gx[...], wgu[xx]).astype(BF)
            send(ps.at[c, i], pr.at[c, i - 1], s_rs, r_rs.at[c], tensor=yl * 4 + xx)
        ps[c, 0] = nn(gx[...], wgu[x]).astype(BF)

    def activate(c):
        wait(ss_r.at[c], r_ss.at[c])
        wait(pr.at[c], r_rs.at[c])
        squares = ss_s[c, 0:1] + ss_r[c, 0, 0:1] + ss_r[c, 1, 0:1] + ss_r[c, 2, 0:1]
        inverse = lax.rsqrt(squares * (1.0 / 4096.0) + 1e-06)
        eye = iota((ROWS, ROWS), 0) == iota((ROWS, ROWS), 1)
        inverse = jnp.sum(jnp.where(eye, inverse, 0.0), axis=1, keepdims=True)
        sums = ps[c, 0].astype(F32) + pr[c, 0].astype(F32) + pr[c, 1].astype(F32) + pr[c, 2].astype(F32)
        sums = sums * inverse
        gated, upped = sums[:, :128], sums[:, 128:]
        activation = (gated / (1.0 + jnp.exp(-gated)) * upped).astype(BF)
        act_s[c] = activation
        mine = pl.ds(pl.multiple_of(t * 128, 128), 128)
        act_r[c, :, mine] = activation
        for i in range(1, 8):
            send(act_s.at[c], act_r.at[c, :, mine], s_act, r_act.at[c], tensor=lax.rem(t + i, 8))

    def produce(c):
        if c == 0:
            local[2].wait()
        wait(act_r.at[c, :, pl.ds(0, 896)], r_act.at[c])
        ob[PER * c : PER * c + PER] = nn(act_r[c], dw[...]).astype(BF).reshape(PER, 2, 16, 512)
        for p in range(PER * c, PER * c + PER):
            zz = lax.rem(z - offset_of(p) + 16, 16)
            dst = rb.at[2 * p + yh]
            if p == 0:
                rb[yh] = ob[0, yh]
                send(ob.at[0, 1 - yh], dst, s_ret, r_ret, expert=far)
            else:
                for oy in range(2):
                    send(ob.at[p, oy], dst, s_ret, r_ret, expert=oy * 16 + zz)

    for turn in range(CHUNKS + 4):
        if turn < CHUNKS:
            forward(turn)
        if 0 <= turn - 1 < CHUNKS:
            project(turn - 1)
        if 0 <= turn - 2 < CHUNKS:
            activate(turn - 2)
        if 0 <= turn - 3 < CHUNKS:
            produce(turn - 3)

    weight = pick[yh].astype(F32).reshape(32, 16, 128) * wt[...].reshape(32, 1, 128)
    weight = weight.reshape(512, 128)
    high = weight.astype(BF)
    low = (weight - high.astype(F32)).astype(BF)
    wait(rb.at[pl.ds(0, 31)], r_ret)
    back = rb[...].reshape(512, 512)
    out[0] = (tn(high, back) + tn(low, back)).astype(BF)

    for copy in sends:
        copy.wait_send()
    wait(wgu.at[pl.ds(0, 3)], s_gu)
    wait(info_r.at[pl.ds(0, 31)], s_info)
    wait(p2r.at[pl.ds(0, 7)], s_p2)
    wait(img_r.at[pl.ds(0, 15)], s_img)
    wait(xr.at[pl.ds(0, 15)], s_disp)
    wait(xk.at[pl.ds(0, 12)], s_ag)
    wait(pr, s_rs)
    wait(ss_r, s_ss)
    wait(act_r.at[:, :, pl.ds(0, 896)], s_act)
    wait(rb.at[pl.ds(0, 31)], s_ret)


def body(
    patches, patch_gain, patch_bias, first_weight, first_bias, second_weight, second_bias,
    image_units, image_owner, image_offset, text_states, token_gain, expert_ids,
    route_weights, gate_weight, up_weight, down_weight,
):
    vmem = pl.BlockSpec(memory_space=pltpu.VMEM)
    anywhere = pl.BlockSpec(memory_space=pl.ANY)
    dma = pltpu.SemaphoreType.DMA
    scratch = [
        pltpu.VMEM((16, 144, 384), BF),
        pltpu.VMEM((16, 128, 384), BF),
        pltpu.VMEM((2, 64, 2304), BF),
        pltpu.VMEM((2, 64, 2304), BF),
        pltpu.VMEM((1, 384), F32),
        pltpu.VMEM((128, 384), BF),
        pltpu.VMEM((128, 384), BF),
        pltpu.VMEM((128, 384), BF),
        pltpu.VMEM((7, 128, 256), BF),
        pltpu.VMEM((7, 128, 256), BF),
        pltpu.VMEM((128, 128), BF),
        pltpu.VMEM((128, 128), BF),
        pltpu.VMEM((16, 8, 128), F32),
        pltpu.VMEM((32, 8, 128), F32),
        pltpu.VMEM((16, 16, 128), BF),
        pltpu.VMEM((16, 16, 128), BF),
        pltpu.VMEM((2, 128, 256), BF),
        pltpu.VMEM((2, 32, 128), BF),
        pltpu.VMEM((32, 128), F32),
        pltpu.VMEM((2, 512, 128), BF),
        pltpu.VMEM((2, 128, 256), BF),
        pltpu.VMEM((16, 2, 32, 256), BF),
        pltpu.VMEM((16, 2, 32, 256), BF),
        pltpu.VMEM((16, 4, 32, 256), BF),
        pltpu.VMEM((4, 1024, 256), BF),
        pltpu.VMEM((1024, 512), BF),
        pltpu.VMEM((ROWS, 1024), BF),
        pltpu.VMEM((CHUNKS, 4, ROWS, 256), BF),
        pltpu.VMEM((CHUNKS, 3, ROWS, 256), BF),
        pltpu.VMEM((CHUNKS, 8, ROWS), F32),
        pltpu.VMEM((CHUNKS, 3, 8, ROWS), F32),
        pltpu.VMEM((CHUNKS, ROWS, 128), BF),
        pltpu.VMEM((CHUNKS, ROWS, 1024), BF),
        pltpu.VMEM((16, 2, 16, 512), BF),
        pltpu.VMEM((32, 16, 512), BF),
        dma((2, 8)), dma((2, 8)), dma((2, 7)), dma((2, 7)),
        dma((7,)), dma, dma, dma((5,)), dma((5,)),
        dma, dma, dma, dma, dma, dma,
        dma, dma((16,)), dma, dma((CHUNKS,)),
        dma, dma((CHUNKS,)), dma, dma((CHUNKS,)), dma, dma((CHUNKS,)),
        dma, dma,
    ]
    call = pl.pallas_call(
        kernel,
        out_shape=jax.ShapeDtypeStruct((1, 128, 512), BF),
        in_specs=[
            anywhere, vmem, vmem, vmem, vmem, vmem, vmem, vmem, vmem, vmem, anywhere, vmem,
            vmem, vmem, anywhere, anywhere, anywhere,
        ],
        out_specs=vmem,
        scratch_shapes=scratch,
        compiler_params=pltpu.CompilerParams(
            collective_id=0, has_side_effects=True, vmem_limit_bytes=48 * 1024 * 1024
        ),
    )
    return call(
        patches, patch_gain[None], patch_bias[None], first_weight, first_bias[None],
        second_weight, second_bias[None], image_units, image_owner, image_offset,
        text_states, token_gain[None], expert_ids[0], route_weights[0],
        gate_weight, up_weight, down_weight,
    )


def solution(mesh):
    in_specs = (
        P(("dp", "expert"), None, None),
        P(),
        P(),
        P("expert", "tensor"),
        P("tensor"),
        P("expert", "tensor"),
        P(),
        P(("dp", "expert"), None),
        P(("dp", "expert"), None),
        P(("dp", "expert"), None),
        P(("dp", "expert"), None, None),
        P(),
        P(("dp", "expert"), None, None),
        P(("dp", "expert"), None, None),
        P("expert", None, "tensor"),
        P("expert", None, "tensor"),
        P("expert", None, "tensor"),
    )
    out_specs = P(("dp", "expert"), None, "tensor")
    return jax.shard_map(body, mesh=mesh, in_specs=in_specs, out_specs=out_specs, check_vma=False)
```

time: 768 us -> 139 us (0.18)
  the two profiles are of different devices: /device:TPU:32 before, /device:TPU:2 now
where the time goes in v1:
time: 139 us; the launch traced here: 138 us
  Pallas kernels  128 us (92%)
  local copies, waits for them, and re-layouts  10.3 us (7%)
    pallas_call x1, Pallas kernels, body(): call(patches, patch_gain[None], patch_bias[None], first_weight, first_bia...  128 us
    unnamed x36, local copies, waits for them, and re-layouts  9.57 us

profile of v1, /device:TPU:2, one launch (start us, length us, event | category | flops | bytes accessed | tf_op | source)
XLA Modules:
  0.0 138.2 jit_solution(586768211190272604)
XLA Ops:
  0.0 0.7 copy-done.15
  0.7 0.7 broadcast_in_dim.15.pgain
  1.4 0.0 copy-done.12
  1.4 0.7 copy-done.13
  2.1 0.1 copy.18
  2.2 0.0 copy-done.14
  2.2 0.0 copy-start.5
  2.2 0.1 copy.19
  2.3 0.7 copy-done.11
  3.0 0.0 copy-start.10
  3.0 0.1 copy.20.w2
  3.1 0.0 copy-done.5
  3.1 0.6 copy-done.6
  3.7 0.0 copy-done.7
  3.7 0.0 copy-done.8
  3.7 0.0 copy-done.9
  3.7 0.0 copy-done.10
  3.7 1.2 copy-done
  5.0 1.2 copy-done.1
  6.2 1.2 copy-done.2
  7.4 1.2 copy-done.3
  8.6 1.1 copy-done.4
  9.7 127.9 %shard_map.163 = bf16[1,128,512]{2,1,0:T(8,128)(2,1)S(1)} custom-call(bf16[1,64,4608]{2,1,0:T(8,128)(2,1)S(1)} %copy-done.4, f32[1,1152]{1,0:T(1,128)S(1)} %broadcast_in_dim.15.pgain, f32[1,1152]{1,0:T(1,128)S(1)} %broadcast_in_dim.16.pbias, bf16[144,288]{1,0:T(8,128)(2,1)S(1)} %copy-done.5, f32[1,288]{1,0:T(1,128)S(1)} %broadcast_in_dim.17.b1, ...), custom_call_target="tpu_custom_call" | custom-call | tf_op jit(solution)/shard_map/pallas_call | solution.py:439
  137.6 0.7 copy.22
  (16 shorter events, 0.0 us)
Async XLA Ops:
  0.0 0.7 copy-start.15
  0.7 0.7 copy-start.12
  1.4 0.7 copy-start.13
  1.4 0.8 copy-start.14
  2.1 0.9 copy-start.11
  2.2 0.9 copy-start.5
  3.0 0.7 copy-start.6
  3.0 0.7 copy-start.7
  3.0 0.7 copy-start.8
  3.0 0.7 copy-start.9
  3.0 0.7 copy-start.10
  3.7 1.2 copy-start
  5.0 1.2 copy-start.1
  6.2 1.2 copy-start.2
  7.4 1.2 copy-start.3
  8.6 1.1 copy-start.4

commit v2 on v1

--- a/solution.py
+++ b/solution.py
@@ -16,10 +16,8 @@
 ROWS = PER * 32
 
 
-def offset_of(place):
-    if place == 0:
-        return 0
-    return (place + 1) // 2 if place % 2 else PLANES - place // 2
+DISTANCES = (5, 11, 4, 12, 6, 10, 3, 13, 7, 9, 2, 14, 8, 1, 15, 0)
+HERE = DISTANCES.index(0)
 
 
 def nn(a, b):
@@ -42,7 +40,7 @@
     patches, pgain, pbias, w1, b1, w2, b2, units, owners, offsets, text, tgain,
     ids, shares, gate, up, down,
     out,
-    g1, g2, pv, xn, b1p, hid, p1s, p1r, p2s, p2r, sel_own, sel_far, info_s, info_r,
+    g1, g2, w1x, pv, xn, hid, p1s, p1r, p2s, p2r, sel_own, sel_far, info_own, info_far, info_s, info_r,
     img_s, img_r, tx, rt, wt, pick, st, xs, xr, xk, wgu, dw, gx, ps, pr, ss_s, ss_r,
     act_s, act_r, ob, rb,
     s_w, r_w, s_c, r_c, l_sem, s_gu, r_gu, s_one, r_one, s_info, r_info, s_p2, r_p2,
@@ -57,7 +55,6 @@
     y = 2 * yh + yl
     far = (1 - yh) * 16 + z
     col = yh * 2048 + x * 512 + yl * 256
-    far_col = (1 - yh) * 2048 + x * 512 + yl * 256
 
     def send(src, dst, ssem, rsem, **dev):
         copy = pltpu.make_async_remote_copy(
@@ -81,66 +78,108 @@
         copy.start()
 
     barrier = pltpu.get_barrier_semaphore()
+    after = yh * 16 + lax.rem(z + 1, 16)
+    ahead = yh * 16 + lax.rem(z + 15, 16)
+    across = lax.rem(t + 4, 8)
 
     def greet(**dev):
         pl.semaphore_signal(barrier, inc=1, device_id=dev, device_id_type=MESH)
 
-    for i in range(1, 32):
-        greet(expert=lax.rem(e + i, 32))
+    greet(expert=after)
+    greet(expert=ahead)
+    greet(dp=1 - core)
     for i in range(1, 8):
         greet(tensor=lax.rem(t + i, 8))
-    greet(dp=1 - core)
-    greet(expert=far, tensor=lax.rem(t + 4, 8))
-
-    g1[z, :, 256:] = jnp.zeros((144, 128), BF)
-    g2[z, :, 256:] = jnp.zeros((128, 128), BF)
-    g1[z, :, :288] = w1[...]
-    g2[z, :, :288] = w2[...]
-    b1p[...] = jnp.zeros((1, 384), F32)
-    b1p[:, :288] = b1[...]
-
-    pl.semaphore_wait(barrier, 40)
-
-    step_z = 1 - 2 * core
-    nxt = yh * 16 + lax.rem(z + step_z + 16, 16)
-    sends = []
+    greet(expert=far)
+    greet(expert=far, tensor=across)
+
+    g1[z, :144, :] = w1[:, :256]
+    for r in range(9):
+        low = 144 if r < 8 else 160
+        g1[z, low : low + 16, 32 * (r % 8) : 32 * (r % 8) + 32] = w1[16 * r : 16 * r + 16, 256:288]
+    g2[z] = w2[...]
+
+    pl.semaphore_wait(barrier, 12)
+
+    sends, drains = [], []
+
+    def finish():
+        for copy in sends:
+            copy.wait_send()
+        for ref, sem in drains:
+            wait(ref, sem)
+
+        @pl.when(core == 1)
+        def _():
+            for w, g in enumerate(gathered):
+                wait(g.at[pl.ds(0, 15)], s_w.at[w])
+                wait(g.at[pl.ds(0, 15)], s_c.at[w])
+
     gathered = (g1, g2)
-    for w, g in enumerate(gathered):
-        sends.append(send(g.at[z], g.at[z], s_w.at[w, 0], r_w.at[w, 0], expert=nxt))
+
+    def ring(step):
+        if step >= 0:
+            for w, g in enumerate(gathered):
+                for way, to in enumerate((after, ahead)):
+                    if step == 7 and way == 1:
+                        continue
+                    origin = lax.rem(z + (15 - step if way == 0 else step + 1), 16)
+                    block = g.at[origin]
+                    wait(block, r_w.at[w, way, step])
+                    if step < 7 - way:
+                        send(block, block, s_w.at[w], r_w.at[w, way, step + 1], expert=to)
+                    send(block, block, s_c.at[w], r_c.at[w], dp=0)
+        else:
+            for w, g in enumerate(gathered):
+                for way, to in enumerate((after, ahead)):
+                    send(g.at[z], g.at[z], s_w.at[w], r_w.at[w, way, 0], expert=to)
+
+    @pl.when(core == 1)
+    def _():
+        ring(-1)
+
     far_half = pl.ds(pl.multiple_of(2304 * (1 - yh), 128), 2304)
-    sends.append(send(patches.at[0, :, far_half], pv.at[yh], s_one.at[0], r_one.at[0], expert=far))
-    far_cols = pl.ds(pl.multiple_of(far_col, 128), 256)
-    sends.append(send(text.at[0, :, far_cols], tx.at[yh], s_one.at[1], r_one.at[1], expert=far))
-    for i in range(1, 4):
-        xx = lax.rem(x + i, 4)
-        for h in range(2):
-            rows = pl.ds(pl.multiple_of(2048 * h + 512 * xx, 512), 512)
-            for k, source in enumerate((gate, up)):
-                send(
-                    source.at[0, rows, :],
-                    wgu.at[x, pl.ds(512 * h, 512), pl.ds(128 * k, 128)],
-                    s_gu, r_gu, tensor=yl * 4 + xx,
-                )
+    sends.append(
+        send(patches.at[0, :, far_half], pv.at[yh], s_one.at[0], r_one.at[0], expert=far, tensor=across)
+    )
+
+    def regroup():
+        for i in range(1, 4):
+            xx = lax.rem(x + i, 4)
+            for h in range(2):
+                rows = pl.ds(pl.multiple_of(2048 * h + 512 * xx, 512), 512)
+                for k, source in enumerate((gate, up)):
+                    send(
+                        source.at[0, rows, :],
+                        wgu.at[x, pl.ds(512 * h, 512), pl.ds(128 * k, 128)],
+                        s_gu, r_gu, tensor=yl * 4 + xx,
+                    )
+        drains.append((wgu.at[pl.ds(0, 3)], s_gu))
+        cols = pl.ds(pl.multiple_of((1 - yh) * 2048 + x * 512 + (1 - yl) * 256, 128), 256)
+        sends.append(
+            send(text.at[0, :, cols], tx.at[yh], s_one.at[1], r_one.at[1], expert=far, tensor=across)
+        )
 
     def iota(shape, dim):
         return lax.broadcasted_iota(I32, shape, dim)
 
     def route():
-        lane = iota((128, 128), 1)
-        place = lane >> 1
-        dist = jnp.where((place & 1) == 1, (place + 1) >> 1, (16 - (place >> 1)) & 15)
-        expert = jnp.where(lane < 32, (lane & 1) * 16 + ((z + dist) & 15), -1)
-        member = jnp.zeros((128, 128), F32)
-        share = jnp.zeros((128, 128), F32)
+        line = iota((32, 128), 0)
+        dist = jnp.zeros((32, 128), I32)
+        for p, d in enumerate(DISTANCES):
+            dist = jnp.where((line >> 1) == p, d, dist)
+        expert = (line & 1) * 16 + ((z + dist) & 15)
+        member = jnp.zeros((32, 128), F32)
+        share = jnp.zeros((32, 128), F32)
         for k in range(8):
-            named = ids[:, k : k + 1] == expert
+            named = ids[k : k + 1, :] == expert
             member = jnp.where(named, 1.0, member)
-            share = share + jnp.where(named, shares[:, k : k + 1], 0.0)
-        before = (iota((128, 128), 1) < iota((128, 128), 0)).astype(F32).astype(BF)
-        rank = nn(before, member.astype(BF))
-        rt[yh] = jnp.where(member > 0.5, rank, -1.0).T[:32].astype(BF)
-        wt[...] = share.T[:32]
-        sends.append(send(rt.at[yh], rt.at[yh], s_one.at[2], r_one.at[2], expert=far))
+            share = share + jnp.where(named, shares[k : k + 1, :], 0.0)
+        before = (iota((128, 128), 0) < iota((128, 128), 1)).astype(F32).astype(BF)
+        rank = nn(member.astype(BF), before)
+        rt[yh] = jnp.where(member > 0.5, rank, -1.0).astype(BF)
+        wt[...] = share
+        sends.append(send(rt.at[yh], rt.at[yh], s_one.at[2], r_one.at[2], expert=far, tensor=across))
 
     def images():
         unit_row = units[...].astype(F32)
@@ -162,29 +201,23 @@
         source = jnp.where(valid, base + start + turn, -1.0)
         position = jnp.where(valid, ((column >> 1) & 1).astype(F32) * 128.0 + offset + turn, -1.0)
         sel_own[...] = (iota((128, 128), 1).astype(F32) == source).astype(F32).astype(BF)
-        info_s[...] = jnp.broadcast_to(position, (128, 128)).reshape(16, 8, 128)
-        info_r[yh * 16] = info_s[0]
-        sends.append(send(sel_own, sel_far, s_one.at[3], r_one.at[3], expert=far))
-        for d in range(16):
-            zz = lax.rem(z + d, 16)
-            dst = info_r.at[yh * 16 + d]
-            send(info_s.at[d], dst, s_info, r_info, expert=(1 - yh) * 16 + zz)
-            if d > 0:
-                send(info_s.at[d], dst, s_info, r_info, expert=yh * 16 + zz)
-
-    def norm_patches(own):
+        info_own[...] = jnp.broadcast_to(position, (128, 128)).reshape(16, 8, 128)
+        sends.append(send(sel_own, sel_far, s_one.at[3], r_one.at[3], expert=far, tensor=across))
+        sends.append(send(info_own, info_far, s_one.at[5], r_one.at[5], expert=far, tensor=across))
+
+    def norm_patches(own, p):
         g = yh if own else 1 - yh
-        if own:
-            local[0].wait()
-        else:
-            wait(pv.at[g], r_one.at[0])
-        for p in range(2):
-            part = pl.ds(1152 * p, 1152)
-            v = pv[g, :, part].astype(F32)
-            center = v - jnp.mean(v, axis=1, keepdims=True)
-            variance = jnp.mean(center * center, axis=1, keepdims=True)
-            scaled = center * lax.rsqrt(variance + 1e-06) * pgain[...] + pbias[...]
-            xn[g, :, part] = scaled.astype(BF)
+        if p == 0:
+            if own:
+                local[0].wait()
+            else:
+                wait(pv.at[g], r_one.at[0])
+        part = pl.ds(1152 * p, 1152)
+        v = pv[g, :, part].astype(F32)
+        center = v - jnp.mean(v, axis=1, keepdims=True)
+        variance = jnp.mean(center * center, axis=1, keepdims=True)
+        scaled = center * lax.rsqrt(variance + 1e-06) * pgain[...] + pbias[...]
+        xn[g, :, part] = scaled.astype(BF)
 
     def selections():
         wait(rt.at[1 - yh], r_one.at[2])
@@ -194,48 +227,72 @@
             pick[oy] = (ranks == slots).astype(F32).reshape(512, 128).astype(BF)
 
     jobs = {
-        0: [route, images],
-        1: [lambda: norm_patches(True)],
-        2: [lambda: norm_patches(False)],
-        3: [selections],
+        0: [regroup, route],
+        1: [images],
+        2: [lambda: norm_patches(True, 0)],
+        3: [lambda: norm_patches(True, 1)],
+        4: [selections],
+        5: [lambda: norm_patches(False, 0)],
+        6: [lambda: norm_patches(False, 1)],
     }
     for s in range(8):
-        origin = lax.rem(z - step_z * (s + 1) + 32, 16)
-        for w, g in enumerate(gathered):
-            wait(g.at[origin], r_w.at[w, s])
-            if s < 7:
-                block = g.at[origin]
-                sends.append(send(block, block, s_w.at[w, s + 1], r_w.at[w, s + 1], expert=nxt))
-                sends.append(send(block, block, s_c.at[w, s], r_c.at[w, s], dp=1 - core))
+
+        @pl.when(core == 1)
+        def _():
+            ring(s)
+
         for job in jobs.get(s, ()):
             job()
 
-    def other_core(w):
-        for s in range(7):
-            origin = lax.rem(z + step_z * (s + 1) + 32, 16)
-            wait(gathered[w].at[origin], r_c.at[w, s])
-
-    other_core(0)
-    part1 = nn(xn[...].reshape(128, 2304), g1[...].reshape(2304, 384))
-    p1s[...] = part1.astype(BF)
+    @pl.when(core == 0)
+    def _():
+        wait(g1.at[pl.ds(0, 15)], r_c.at[0])
+
+    w1x[...] = jnp.zeros((16, 144, 128), BF)
+    for r in range(9):
+        low = 144 if r < 8 else 160
+        w1x[:, 16 * r : 16 * r + 16, :32] = g1[:, low : low + 16, 32 * (r % 8) : 32 * (r % 8) + 32]
+    rows = xn[...].reshape(128, 2304)
+    main = nn(rows, g1[:, :144, :].reshape(2304, 256))
+    tail = nn(rows, w1x[...].reshape(2304, 128))
+    p1s[:128] = main.astype(BF)
+    for r in range(8):
+        p1s[128:144, 32 * r : 32 * r + 32] = tail[16 * r : 16 * r + 16, :32].astype(BF)
     sends.append(send(p1s, p1r, s_one.at[4], r_one.at[4], expert=far))
-    other_core(1)
+
+    @pl.when(core == 0)
+    def _():
+        wait(g2.at[pl.ds(0, 15)], r_c.at[1])
+
+    wait(sel_far, r_one.at[3])
+    wait(info_far, r_one.at[5])
+    chosen = sel_own[...] + sel_far[...]
+    info_s[...] = jnp.maximum(info_own[...], info_far[...])
+
+    def gelu(v):
+        return (0.5 * v * (1.0 + lax.erf(v * (0.5**0.5)))).astype(BF)
+
     wait(p1r, r_one.at[4])
-    v = part1 + p1r[...].astype(F32) + b1p[...]
-    hid[...] = (0.5 * v * (1.0 + lax.erf(v * (0.5**0.5)))).astype(BF)
+    hid[:, :256] = gelu(main + p1r[:128].astype(F32) + b1[:, :256])
+    for r in range(8):
+        far_tail = p1r[128:144, 32 * r : 32 * r + 32].astype(F32)
+        hid[16 * r : 16 * r + 16, 256:] = gelu(tail[16 * r : 16 * r + 16, :32] + far_tail + b1[:, 256:])
 
     def second(tt):
         k = 2 * lax.rem(tt, 4) + tt // 4
-        return nt(hid[...], g2[pl.ds(2 * k, 2)].reshape(256, 384))
+        units_here = hid[...]
+        return jnp.concatenate([nn(units_here, g2[2 * k]), nn(units_here, g2[2 * k + 1])], axis=1)
 
     for i in range(1, 8):
         tt = lax.rem(t + i, 8)
         p2s[i - 1] = second(tt).astype(BF)
         send(p2s.at[i - 1], p2r.at[i - 1], s_p2, r_p2, tensor=tt)
+    drains.append((p2r.at[pl.ds(0, 7)], s_p2))
     total = second(t) + b2[:, pl.ds(pl.multiple_of(col, 128), 256)]
-    wait(info_r.at[pl.ds(0, 31)], r_info)
-    wait(sel_far, r_one.at[3])
-    chosen = sel_own[...] + sel_far[...]
+    for d in range(1, 16):
+        send(info_s.at[d], info_r.at[d], s_info, r_info, expert=yh * 16 + lax.rem(z + d, 16))
+    info_r[0] = info_s[0]
+    drains.append((info_r.at[pl.ds(0, 15)], s_info))
     wait(p2r.at[pl.ds(0, 7)], r_p2)
     for i in range(7):
         total = total + p2r[i].astype(F32)
@@ -247,9 +304,11 @@
     for d in range(1, 16):
         send(img_s.at[d], img_r.at[d], s_img, r_img, expert=yh * 16 + lax.rem(z + d, 16))
 
+    drains.append((img_r.at[pl.ds(0, 15)], s_img))
     local[1].wait()
     wait(tx.at[1 - yh], r_one.at[1])
-    position = jnp.maximum(info_r[pl.ds(0, 16)], info_r[pl.ds(16, 16)])
+    wait(info_r.at[pl.ds(0, 15)], r_info)
+    position = info_r[...]
     blank = jnp.zeros((16, 8, 128), F32)
     placed = []
     for oy in range(2):
@@ -269,19 +328,23 @@
 
     for oy in range(2):
         xs[:, :, 16 * oy : 16 * oy + 16, :] = nn(pick[oy], st[oy]).astype(BF).reshape(16, 2, 16, 256)
-    for p in range(1, 16):
-        send(xs.at[p], xr.at[p], s_disp, r_disp.at[p], expert=yh * 16 + lax.rem(z + offset_of(p), 16))
+    for p in range(16):
+        if p == HERE:
+            continue
+        send(xs.at[p], xr.at[p], s_disp, r_disp.at[p], expert=yh * 16 + lax.rem(z + DISTANCES[p], 16))
+
+    drains.append((xr.at[pl.ds(0, 15)], s_disp))
 
     def forward(c):
         for p in range(PER * c, PER * c + PER):
-            if p > 0:
+            if p != HERE:
                 wait(xr.at[p], r_disp.at[p])
-            block = xs.at[p] if p == 0 else xr.at[p]
+            block = xs.at[p] if p == HERE else xr.at[p]
             xk[p, y] = block[yh]
             dst = xk.at[p, y]
-            send(block.at[yh], dst, s_ag, r_ag.at[c], tensor=lax.rem(t + 4, 8))
+            send(block.at[yh], dst, s_ag, r_ag.at[c], tensor=across)
             send(block.at[1 - yh], dst, s_ag, r_ag.at[c], expert=far)
-            send(block.at[1 - yh], dst, s_ag, r_ag.at[c], expert=far, tensor=lax.rem(t + 4, 8))
+            send(block.at[1 - yh], dst, s_ag, r_ag.at[c], expert=far, tensor=across)
 
     def project(c):
         wait(xk.at[pl.ds(PER * c, 3)], r_ag.at[c])
@@ -331,11 +394,11 @@
         wait(act_r.at[c, :, pl.ds(0, 896)], r_act.at[c])
         ob[PER * c : PER * c + PER] = nn(act_r[c], dw[...]).astype(BF).reshape(PER, 2, 16, 512)
         for p in range(PER * c, PER * c + PER):
-            zz = lax.rem(z - offset_of(p) + 16, 16)
+            zz = lax.rem(z - DISTANCES[p] + 16, 16)
             dst = rb.at[2 * p + yh]
-            if p == 0:
-                rb[yh] = ob[0, yh]
-                send(ob.at[0, 1 - yh], dst, s_ret, r_ret, expert=far)
+            if p == HERE:
+                rb[2 * p + yh] = ob[p, yh]
+                send(ob.at[p, 1 - yh], dst, s_ret, r_ret, expert=far)
             else:
                 for oy in range(2):
                     send(ob.at[p, oy], dst, s_ret, r_ret, expert=oy * 16 + zz)
@@ -350,6 +413,11 @@
         if 0 <= turn - 3 < CHUNKS:
             produce(turn - 3)
 
+    drains.append((xk.at[pl.ds(0, 12)], s_ag))
+    drains.append((pr, s_rs))
+    drains.append((ss_r, s_ss))
+    drains.append((act_r.at[:, :, pl.ds(0, 896)], s_act))
+    drains.append((rb.at[pl.ds(0, 31)], s_ret))
     weight = pick[yh].astype(F32).reshape(32, 16, 128) * wt[...].reshape(32, 1, 128)
     weight = weight.reshape(512, 128)
     high = weight.astype(BF)
@@ -358,18 +426,7 @@
     back = rb[...].reshape(512, 512)
     out[0] = (tn(high, back) + tn(low, back)).astype(BF)
 
-    for copy in sends:
-        copy.wait_send()
-    wait(wgu.at[pl.ds(0, 3)], s_gu)
-    wait(info_r.at[pl.ds(0, 31)], s_info)
-    wait(p2r.at[pl.ds(0, 7)], s_p2)
-    wait(img_r.at[pl.ds(0, 15)], s_img)
-    wait(xr.at[pl.ds(0, 15)], s_disp)
-    wait(xk.at[pl.ds(0, 12)], s_ag)
-    wait(pr, s_rs)
-    wait(ss_r, s_ss)
-    wait(act_r.at[:, :, pl.ds(0, 896)], s_act)
-    wait(rb.at[pl.ds(0, 31)], s_ret)
+    finish()
 
 
 def body(
@@ -378,23 +435,25 @@
     route_weights, gate_weight, up_weight, down_weight,
 ):
     vmem = pl.BlockSpec(memory_space=pltpu.VMEM)
-    anywhere = pl.BlockSpec(memory_space=pl.ANY)
+    hbm = pl.BlockSpec(memory_space=pltpu.HBM)
     dma = pltpu.SemaphoreType.DMA
     scratch = [
-        pltpu.VMEM((16, 144, 384), BF),
-        pltpu.VMEM((16, 128, 384), BF),
+        pltpu.VMEM((16, 176, 256), BF),
+        pltpu.VMEM((16, 288, 128), BF),
+        pltpu.VMEM((16, 144, 128), BF),
         pltpu.VMEM((2, 64, 2304), BF),
         pltpu.VMEM((2, 64, 2304), BF),
-        pltpu.VMEM((1, 384), F32),
-        pltpu.VMEM((128, 384), BF),
-        pltpu.VMEM((128, 384), BF),
-        pltpu.VMEM((128, 384), BF),
+        pltpu.VMEM((128, 288), BF),
+        pltpu.VMEM((144, 256), BF),
+        pltpu.VMEM((144, 256), BF),
         pltpu.VMEM((7, 128, 256), BF),
         pltpu.VMEM((7, 128, 256), BF),
         pltpu.VMEM((128, 128), BF),
         pltpu.VMEM((128, 128), BF),
         pltpu.VMEM((16, 8, 128), F32),
-        pltpu.VMEM((32, 8, 128), F32),
+        pltpu.VMEM((16, 8, 128), F32),
+        pltpu.VMEM((16, 8, 128), F32),
+        pltpu.VMEM((16, 8, 128), F32),
         pltpu.VMEM((16, 16, 128), BF),
         pltpu.VMEM((16, 16, 128), BF),
         pltpu.VMEM((2, 128, 256), BF),
@@ -416,8 +475,8 @@
         pltpu.VMEM((CHUNKS, ROWS, 1024), BF),
         pltpu.VMEM((16, 2, 16, 512), BF),
         pltpu.VMEM((32, 16, 512), BF),
-        dma((2, 8)), dma((2, 8)), dma((2, 7)), dma((2, 7)),
-        dma((7,)), dma, dma, dma((5,)), dma((5,)),
+        dma((2,)), dma((2, 2, 8)), dma((2,)), dma((2,)),
+        dma((7,)), dma, dma, dma((6,)), dma((6,)),
         dma, dma, dma, dma, dma, dma,
         dma, dma((16,)), dma, dma((CHUNKS,)),
         dma, dma((CHUNKS,)), dma, dma((CHUNKS,)), dma, dma((CHUNKS,)),
@@ -427,19 +486,19 @@
         kernel,
         out_shape=jax.ShapeDtypeStruct((1, 128, 512), BF),
         in_specs=[
-            anywhere, vmem, vmem, vmem, vmem, vmem, vmem, vmem, vmem, vmem, anywhere, vmem,
-            vmem, vmem, anywhere, anywhere, anywhere,
+            hbm, vmem, vmem, vmem, vmem, vmem, vmem, vmem, vmem, vmem, hbm, vmem,
+            vmem, vmem, hbm, hbm, hbm,
         ],
         out_specs=vmem,
         scratch_shapes=scratch,
         compiler_params=pltpu.CompilerParams(
-            collective_id=0, has_side_effects=True, vmem_limit_bytes=48 * 1024 * 1024
+            collective_id=0, has_side_effects=True, vmem_limit_bytes=60 * 1024 * 1024
         ),
     )
     return call(
         patches, patch_gain[None], patch_bias[None], first_weight, first_bias[None],
-        second_weight, second_bias[None], image_units, image_owner, image_offset,
-        text_states, token_gain[None], expert_ids[0], route_weights[0],
+        second_weight.T, second_bias[None], image_units, image_owner, image_offset,
+        text_states, token_gain[None], expert_ids[0].T, route_weights[0].T,
         gate_weight, up_weight, down_weight,
     )
 

time: 139 us -> 126 us (0.906)
  the two profiles are of different devices: /device:TPU:2 before, /device:TPU:34 now
where the time goes in v2:
time: 126 us
  Pallas kernels  122 us (97%)
  local copies, waits for them, and re-layouts  4.05 us (3%)
    pallas_call x1, Pallas kernels, body(): call(patches, patch_gain[None], patch_bias[None], first_weight, first_bia...  122 us

profile of v2, /device:TPU:34, one launch (start us, length us, event | category | flops | bytes accessed | tf_op | source)
XLA Modules:
  0.0 126.1 jit_solution(15821408971846629639)
XLA Ops:
  0.0 0.0 copy-start
  0.0 0.0 copy-start.1
  0.0 1.3 %broadcast_in_dim.17.b1 = f32[1,288]{1,0:T(1,128)} reshape(f32[288]{0:T(512)} %param.21) | data formatting | bytes 2304 | tf_op jit(solution)/shard_map/broadcast_in_dim | solution.py:499
  1.3 0.0 copy-done
  1.3 0.6 broadcast_in_dim.15.pgain
  1.9 0.0 copy-done.1
  1.9 0.6 broadcast_in_dim.16.pbias
  2.5 122.1 %shard_map.163 = bf16[1,128,512]{2,1,0:T(8,128)(2,1)} custom-call(bf16[1,64,4608]{2,1,0:T(8,128)(2,1)} %patches.1, f32[1,1152]{1,0:T(1,128)} %broadcast_in_dim.15.pgain, f32[1,1152]{1,0:T(1,128)} %broadcast_in_dim.16.pbias, bf16[144,288]{1,0:T(8,128)(2,1)} %w1.1, f32[1,288]{1,0:T(1,128)} %broadcast_in_dim.17.b1, bf16[288,128]{1,0:T(8,128)(2,1)} %bitcast.9, ...), custom_call_target="tpu_custom_call" | custom-call | tf_op jit(solution)/shard_map/pallas_call | solution.py:498
  124.5 1.6 %copy.19 = bf16[1,128,512]{2,1,0:T(8,128)(2,1)} copy(bf16[1,128,512]{2,1,0:T(8,128)(2,1)} %shard_map.163) | data formatting | bytes 262144
Async XLA Ops:
  0.0 1.3 %copy-start = (f32[1152]{0:T(1024)S(1)}, f32[1152]{0:T(1024)}, u32[]{:S(2)}) copy-start(f32[1152]{0:T(1024)} %param.18) | copy-start | bytes 13828
  0.0 1.9 %copy-start.1 = (f32[1152]{0:T(1024)S(1)}, f32[1152]{0:T(1024)}, u32[]{:S(2)}) copy-start(f32[1152]{0:T(1024)} %param.19) | copy-start | bytes 13828

commit v3 on v2

--- a/solution.py
+++ b/solution.py
@@ -16,7 +16,7 @@
 ROWS = PER * 32
 
 
-DISTANCES = (5, 11, 4, 12, 6, 10, 3, 13, 7, 9, 2, 14, 8, 1, 15, 0)
+DISTANCES = (0, 8, 1, 15, 7, 9, 2, 14, 6, 10, 3, 13, 5, 11, 4, 12)
 HERE = DISTANCES.index(0)
 
 
@@ -40,11 +40,10 @@
     patches, pgain, pbias, w1, b1, w2, b2, units, owners, offsets, text, tgain,
     ids, shares, gate, up, down,
     out,
-    g1, g2, w1x, pv, xn, hid, p1s, p1r, p2s, p2r, sel_own, sel_far, info_own, info_far, info_s, info_r,
-    img_s, img_r, tx, rt, wt, pick, st, xs, xr, xk, wgu, dw, gx, ps, pr, ss_s, ss_r,
-    act_s, act_r, ob, rb,
+    g1, g2, w1x, pv, xz, hid, p1s, p1r, p2s, p2r, swap_own, swap_far, info_s, info_r,
+    img_s, img_r, tx, wt, pick, st, xs, xr, xk, wgu, dw, gx, ps, pr, ss, act_s, act_r, ob, rb,
     s_w, r_w, s_c, r_c, l_sem, s_gu, r_gu, s_one, r_one, s_info, r_info, s_p2, r_p2,
-    s_img, r_img, s_disp, r_disp, s_ag, r_ag, s_rs, r_rs, s_ss, r_ss, s_act, r_act,
+    s_img, r_img, s_disp, r_disp, s_ag, r_ag, s_rs, r_rs, s_act, r_act,
     s_ret, r_ret,
 ):
     e = lax.axis_index("expert")
@@ -69,10 +68,8 @@
         (text.at[0, :, pl.ds(pl.multiple_of(col, 128), 256)], tx.at[yh]),
         (down.at[0], dw),
     ]
-    for h in range(2):
-        rows = pl.ds(pl.multiple_of(2048 * h + 512 * x, 512), 512)
-        local.append((gate.at[0, rows, :], wgu.at[x, pl.ds(512 * h, 512), pl.ds(0, 128)]))
-        local.append((up.at[0, rows, :], wgu.at[x, pl.ds(512 * h, 512), pl.ds(128, 128)]))
+    for k, source in enumerate((gate, up)):
+        local.append((source.at[:, x], wgu.at[x, :, :, pl.ds(128 * k, 128)]))
     local = [pltpu.make_async_copy(a, b, l_sem.at[i]) for i, (a, b) in enumerate(local)]
     for copy in local:
         copy.start()
@@ -93,11 +90,11 @@
     greet(expert=far)
     greet(expert=far, tensor=across)
 
-    g1[z, :144, :] = w1[:, :256]
+    g1[0, :144, :] = w1[:, :256]
     for r in range(9):
         low = 144 if r < 8 else 160
-        g1[z, low : low + 16, 32 * (r % 8) : 32 * (r % 8) + 32] = w1[16 * r : 16 * r + 16, 256:288]
-    g2[z] = w2[...]
+        g1[0, low : low + 16, 32 * (r % 8) : 32 * (r % 8) + 32] = w1[16 * r : 16 * r + 16, 256:288]
+    g2[0] = w2[...]
 
     pl.semaphore_wait(barrier, 12)
 
@@ -112,31 +109,39 @@
         @pl.when(core == 1)
         def _():
             for w, g in enumerate(gathered):
-                wait(g.at[pl.ds(0, 15)], s_w.at[w])
-                wait(g.at[pl.ds(0, 15)], s_c.at[w])
+                wait(g.at[pl.ds(1, 15)], s_w.at[w])
+                wait(g.at[pl.ds(1, 15)], s_c.at[w])
 
     gathered = (g1, g2)
 
+    def hand_on(first, count):
+        for w, g in enumerate(gathered):
+            blocks = g.at[pl.ds(first, count)]
+            send(blocks, blocks, s_c.at[w], r_c.at[w], dp=0)
+
     def ring(step):
-        if step >= 0:
-            for w, g in enumerate(gathered):
-                for way, to in enumerate((after, ahead)):
-                    if step == 7 and way == 1:
-                        continue
-                    origin = lax.rem(z + (15 - step if way == 0 else step + 1), 16)
-                    block = g.at[origin]
-                    wait(block, r_w.at[w, way, step])
-                    if step < 7 - way:
-                        send(block, block, s_w.at[w], r_w.at[w, way, step + 1], expert=to)
-                    send(block, block, s_c.at[w], r_c.at[w], dp=0)
-        else:
-            for w, g in enumerate(gathered):
-                for way, to in enumerate((after, ahead)):
-                    send(g.at[z], g.at[z], s_w.at[w], r_w.at[w, way, 0], expert=to)
+        for w, g in enumerate(gathered):
+            for way, to in enumerate((after, ahead)):
+                if step < 8 - way:
+                    here, there = (step, step + 1) if way == 0 else ((16 - step) % 16, 15 - step)
+                    if step > 0:
+                        wait(g.at[here], r_w.at[w, way, step - 1])
+                    send(g.at[here], g.at[there], s_w.at[w], r_w.at[w, way, step], expert=to)
+                elif step == 8 - way:
+                    here = step if way == 0 else 16 - step
+                    wait(g.at[here], r_w.at[w, way, step - 1])
+        if step == 3:
+            hand_on(1, 3)
+            hand_on(13, 3)
+        if step == 6:
+            hand_on(4, 3)
+            hand_on(10, 3)
+        if step == 8:
+            hand_on(7, 3)
 
     @pl.when(core == 1)
     def _():
-        ring(-1)
+        ring(0)
 
     far_half = pl.ds(pl.multiple_of(2304 * (1 - yh), 128), 2304)
     sends.append(
@@ -146,14 +151,9 @@
     def regroup():
         for i in range(1, 4):
             xx = lax.rem(x + i, 4)
-            for h in range(2):
-                rows = pl.ds(pl.multiple_of(2048 * h + 512 * xx, 512), 512)
-                for k, source in enumerate((gate, up)):
-                    send(
-                        source.at[0, rows, :],
-                        wgu.at[x, pl.ds(512 * h, 512), pl.ds(128 * k, 128)],
-                        s_gu, r_gu, tensor=yl * 4 + xx,
-                    )
+            for k, source in enumerate((gate, up)):
+                dst = wgu.at[x, :, :, pl.ds(128 * k, 128)]
+                send(source.at[:, xx], dst, s_gu, r_gu, tensor=yl * 4 + xx)
         drains.append((wgu.at[pl.ds(0, 3)], s_gu))
         cols = pl.ds(pl.multiple_of((1 - yh) * 2048 + x * 512 + (1 - yl) * 256, 128), 256)
         sends.append(
@@ -177,9 +177,8 @@
             share = share + jnp.where(named, shares[k : k + 1, :], 0.0)
         before = (iota((128, 128), 0) < iota((128, 128), 1)).astype(F32).astype(BF)
         rank = nn(member.astype(BF), before)
-        rt[yh] = jnp.where(member > 0.5, rank, -1.0).astype(BF)
+        swap_own[256:288] = jnp.where(member > 0.5, rank, -1.0).astype(BF)
         wt[...] = share
-        sends.append(send(rt.at[yh], rt.at[yh], s_one.at[2], r_one.at[2], expert=far, tensor=across))
 
     def images():
         unit_row = units[...].astype(F32)
@@ -200,10 +199,9 @@
         base = (yh * 64).astype(F32)
         source = jnp.where(valid, base + start + turn, -1.0)
         position = jnp.where(valid, ((column >> 1) & 1).astype(F32) * 128.0 + offset + turn, -1.0)
-        sel_own[...] = (iota((128, 128), 1).astype(F32) == source).astype(F32).astype(BF)
-        info_own[...] = jnp.broadcast_to(position, (128, 128)).reshape(16, 8, 128)
-        sends.append(send(sel_own, sel_far, s_one.at[3], r_one.at[3], expert=far, tensor=across))
-        sends.append(send(info_own, info_far, s_one.at[5], r_one.at[5], expert=far, tensor=across))
+        swap_own[:128] = (iota((128, 128), 1).astype(F32) == source).astype(F32).astype(BF)
+        swap_own[128:256] = jnp.broadcast_to(position, (128, 128)).astype(BF)
+        sends.append(send(swap_own, swap_far, s_one.at[2], r_one.at[2], expert=far, tensor=across))
 
     def norm_patches(own, p):
         g = yh if own else 1 - yh
@@ -217,14 +215,17 @@
         center = v - jnp.mean(v, axis=1, keepdims=True)
         variance = jnp.mean(center * center, axis=1, keepdims=True)
         scaled = center * lax.rsqrt(variance + 1e-06) * pgain[...] + pbias[...]
-        xn[g, :, part] = scaled.astype(BF)
+        for o in range(8):
+            xz[8 * p + o, g] = scaled[:, 144 * o : 144 * o + 144].astype(BF)
 
     def selections():
-        wait(rt.at[1 - yh], r_one.at[2])
-        for oy in range(2):
-            ranks = rt[oy].astype(F32).reshape(32, 1, 128)
+        wait(swap_far, r_one.at[2])
+        for oy, swap in ((yh, swap_own), (1 - yh, swap_far)):
+            ranks = swap[256:288].astype(F32).reshape(32, 1, 128)
             slots = iota((32, 16, 128), 1).astype(F32)
             pick[oy] = (ranks == slots).astype(F32).reshape(512, 128).astype(BF)
+        positions = jnp.maximum(swap_own[128:256].astype(F32), swap_far[128:256].astype(F32))
+        info_s[...] = positions.reshape(16, 8, 128)
 
     jobs = {
         0: [regroup, route],
@@ -239,40 +240,43 @@
 
         @pl.when(core == 1)
         def _():
-            ring(s)
+            ring(s + 1)
 
         for job in jobs.get(s, ()):
             job()
 
     @pl.when(core == 0)
     def _():
-        wait(g1.at[pl.ds(0, 15)], r_c.at[0])
+        wait(g1.at[pl.ds(1, 15)], r_c.at[0])
 
     w1x[...] = jnp.zeros((16, 144, 128), BF)
     for r in range(9):
         low = 144 if r < 8 else 160
         w1x[:, 16 * r : 16 * r + 16, :32] = g1[:, low : low + 16, 32 * (r % 8) : 32 * (r % 8) + 32]
-    rows = xn[...].reshape(128, 2304)
-    main = nn(rows, g1[:, :144, :].reshape(2304, 256))
-    tail = nn(rows, w1x[...].reshape(2304, 128))
+    main, tail = jnp.zeros((128, 256), F32), jnp.zeros((128, 128), F32)
+    for r in range(16):
+        rows = xz[lax.rem(z - r + 16, 16)].reshape(128, 144)
+        main = main + nn(rows, g1[r, :144, :])
+        tail = tail + nn(rows, w1x[r])
     p1s[:128] = main.astype(BF)
     for r in range(8):
         p1s[128:144, 32 * r : 32 * r + 32] = tail[16 * r : 16 * r + 16, :32].astype(BF)
-    sends.append(send(p1s, p1r, s_one.at[4], r_one.at[4], expert=far))
+    sends.append(send(p1s, p1r, s_one.at[3], r_one.at[3], expert=far))
+    for d in range(1, 16):
+        send(info_s.at[d], info_r.at[d], s_info, r_info, expert=yh * 16 + lax.rem(z + d, 16))
+    info_r[0] = info_s[0]
+    drains.append((info_r.at[pl.ds(0, 15)], s_info))
 
     @pl.when(core == 0)
     def _():
-        wait(g2.at[pl.ds(0, 15)], r_c.at[1])
-
-    wait(sel_far, r_one.at[3])
-    wait(info_far, r_one.at[5])
-    chosen = sel_own[...] + sel_far[...]
-    info_s[...] = jnp.maximum(info_own[...], info_far[...])
+        wait(g2.at[pl.ds(1, 15)], r_c.at[1])
+
+    chosen = swap_own[:128] + swap_far[:128]
 
     def gelu(v):
         return (0.5 * v * (1.0 + lax.erf(v * (0.5**0.5)))).astype(BF)
 
-    wait(p1r, r_one.at[4])
+    wait(p1r, r_one.at[3])
     hid[:, :256] = gelu(main + p1r[:128].astype(F32) + b1[:, :256])
     for r in range(8):
         far_tail = p1r[128:144, 32 * r : 32 * r + 32].astype(F32)
@@ -281,7 +285,7 @@
     def second(tt):
         k = 2 * lax.rem(tt, 4) + tt // 4
         units_here = hid[...]
-        return jnp.concatenate([nn(units_here, g2[2 * k]), nn(units_here, g2[2 * k + 1])], axis=1)
+        return jnp.concatenate([nn(units_here, g2[lax.rem(z - 2 * k + 16, 16)]), nn(units_here, g2[lax.rem(z - 2 * k + 15, 16)])], axis=1)
 
     for i in range(1, 8):
         tt = lax.rem(t + i, 8)
@@ -289,10 +293,6 @@
         send(p2s.at[i - 1], p2r.at[i - 1], s_p2, r_p2, tensor=tt)
     drains.append((p2r.at[pl.ds(0, 7)], s_p2))
     total = second(t) + b2[:, pl.ds(pl.multiple_of(col, 128), 256)]
-    for d in range(1, 16):
-        send(info_s.at[d], info_r.at[d], s_info, r_info, expert=yh * 16 + lax.rem(z + d, 16))
-    info_r[0] = info_s[0]
-    drains.append((info_r.at[pl.ds(0, 15)], s_info))
     wait(p2r.at[pl.ds(0, 7)], r_p2)
     for i in range(7):
         total = total + p2r[i].astype(F32)
@@ -336,18 +336,20 @@
     drains.append((xr.at[pl.ds(0, 15)], s_disp))
 
     def forward(c):
+        part = pl.ds(PER * c, PER)
         for p in range(PER * c, PER * c + PER):
-            if p != HERE:
+            if p == HERE:
+                xr[p] = xs[p]
+            else:
                 wait(xr.at[p], r_disp.at[p])
-            block = xs.at[p] if p == HERE else xr.at[p]
-            xk[p, y] = block[yh]
-            dst = xk.at[p, y]
-            send(block.at[yh], dst, s_ag, r_ag.at[c], tensor=across)
-            send(block.at[1 - yh], dst, s_ag, r_ag.at[c], expert=far)
-            send(block.at[1 - yh], dst, s_ag, r_ag.at[c], expert=far, tensor=across)
+        dst = xk.at[part, y]
+        send(xr.at[part, 1 - yh], dst, s_ag, r_ag.at[c], expert=far)
+        send(xr.at[part, 1 - yh], dst, s_ag, r_ag.at[c], expert=far, tensor=across)
+        send(xr.at[part, yh], dst, s_ag, r_ag.at[c], tensor=across)
+        xk[part, y] = xr[part, yh]
 
     def project(c):
-        wait(xk.at[pl.ds(PER * c, 3)], r_ag.at[c])
+        wait(xk.at[pl.ds(PER * c, PER), pl.ds(0, 3)], r_ag.at[c])
         if c == 0:
             for copy in local[3:]:
                 copy.wait()
@@ -363,22 +365,27 @@
             high = square.astype(BF)
             low = (square - high.astype(F32)).astype(BF)
             squares = squares + nt(ones, high) + nt(ones, low)
-        ss_s[c] = squares
+        ss[c] = squares
+        high = squares.astype(BF).astype(F32)
+        squares = jnp.concatenate([high, squares - high], axis=0).astype(BF)
         for i in range(1, 4):
             xx = lax.rem(x + i, 4)
-            send(ss_s.at[c], ss_r.at[c, i - 1], s_ss, r_ss.at[c], tensor=yl * 4 + xx)
-            ps[c, i] = nn(gx[...], wgu[xx]).astype(BF)
+            ps[c, i, :ROWS] = nn(gx[...], wgu[xx].reshape(1024, 256)).astype(BF)
+            ps[c, i, ROWS:, :ROWS] = squares
             send(ps.at[c, i], pr.at[c, i - 1], s_rs, r_rs.at[c], tensor=yl * 4 + xx)
-        ps[c, 0] = nn(gx[...], wgu[x]).astype(BF)
+        ps[c, 0, :ROWS] = nn(gx[...], wgu[x].reshape(1024, 256)).astype(BF)
 
     def activate(c):
-        wait(ss_r.at[c], r_ss.at[c])
         wait(pr.at[c], r_rs.at[c])
-        squares = ss_s[c, 0:1] + ss_r[c, 0, 0:1] + ss_r[c, 1, 0:1] + ss_r[c, 2, 0:1]
+        squares = ss[c, 0:1]
+        sums = ps[c, 0, :ROWS].astype(F32)
+        for i in range(3):
+            both = pr[c, i, ROWS:, :ROWS].astype(F32)
+            squares = squares + both[0:1] + both[8:9]
+            sums = sums + pr[c, i, :ROWS].astype(F32)
         inverse = lax.rsqrt(squares * (1.0 / 4096.0) + 1e-06)
         eye = iota((ROWS, ROWS), 0) == iota((ROWS, ROWS), 1)
         inverse = jnp.sum(jnp.where(eye, inverse, 0.0), axis=1, keepdims=True)
-        sums = ps[c, 0].astype(F32) + pr[c, 0].astype(F32) + pr[c, 1].astype(F32) + pr[c, 2].astype(F32)
         sums = sums * inverse
         gated, upped = sums[:, :128], sums[:, 128:]
         activation = (gated / (1.0 + jnp.exp(-gated)) * upped).astype(BF)
@@ -413,9 +420,8 @@
         if 0 <= turn - 3 < CHUNKS:
             produce(turn - 3)
 
-    drains.append((xk.at[pl.ds(0, 12)], s_ag))
+    drains.append((xk.at[:, pl.ds(0, 3)], s_ag))
     drains.append((pr, s_rs))
-    drains.append((ss_r, s_ss))
     drains.append((act_r.at[:, :, pl.ds(0, 896)], s_act))
     drains.append((rb.at[pl.ds(0, 31)], s_ret))
     weight = pick[yh].astype(F32).reshape(32, 16, 128) * wt[...].reshape(32, 1, 128)
@@ -442,44 +448,40 @@
         pltpu.VMEM((16, 288, 128), BF),
         pltpu.VMEM((16, 144, 128), BF),
         pltpu.VMEM((2, 64, 2304), BF),
-        pltpu.VMEM((2, 64, 2304), BF),
+        pltpu.VMEM((16, 2, 64, 144), BF),
         pltpu.VMEM((128, 288), BF),
         pltpu.VMEM((144, 256), BF),
         pltpu.VMEM((144, 256), BF),
         pltpu.VMEM((7, 128, 256), BF),
         pltpu.VMEM((7, 128, 256), BF),
-        pltpu.VMEM((128, 128), BF),
-        pltpu.VMEM((128, 128), BF),
-        pltpu.VMEM((16, 8, 128), F32),
-        pltpu.VMEM((16, 8, 128), F32),
+        pltpu.VMEM((288, 128), BF),
+        pltpu.VMEM((288, 128), BF),
         pltpu.VMEM((16, 8, 128), F32),
         pltpu.VMEM((16, 8, 128), F32),
         pltpu.VMEM((16, 16, 128), BF),
         pltpu.VMEM((16, 16, 128), BF),
         pltpu.VMEM((2, 128, 256), BF),
-        pltpu.VMEM((2, 32, 128), BF),
         pltpu.VMEM((32, 128), F32),
         pltpu.VMEM((2, 512, 128), BF),
         pltpu.VMEM((2, 128, 256), BF),
         pltpu.VMEM((16, 2, 32, 256), BF),
         pltpu.VMEM((16, 2, 32, 256), BF),
         pltpu.VMEM((16, 4, 32, 256), BF),
-        pltpu.VMEM((4, 1024, 256), BF),
+        pltpu.VMEM((4, 2, 512, 256), BF),
         pltpu.VMEM((1024, 512), BF),
         pltpu.VMEM((ROWS, 1024), BF),
-        pltpu.VMEM((CHUNKS, 4, ROWS, 256), BF),
-        pltpu.VMEM((CHUNKS, 3, ROWS, 256), BF),
+        pltpu.VMEM((CHUNKS, 4, ROWS + 16, 256), BF),
+        pltpu.VMEM((CHUNKS, 3, ROWS + 16, 256), BF),
         pltpu.VMEM((CHUNKS, 8, ROWS), F32),
-        pltpu.VMEM((CHUNKS, 3, 8, ROWS), F32),
         pltpu.VMEM((CHUNKS, ROWS, 128), BF),
         pltpu.VMEM((CHUNKS, ROWS, 1024), BF),
         pltpu.VMEM((16, 2, 16, 512), BF),
         pltpu.VMEM((32, 16, 512), BF),
         dma((2,)), dma((2, 2, 8)), dma((2,)), dma((2,)),
-        dma((7,)), dma, dma, dma((6,)), dma((6,)),
+        dma((5,)), dma, dma, dma((4,)), dma((4,)),
         dma, dma, dma, dma, dma, dma,
         dma, dma((16,)), dma, dma((CHUNKS,)),
-        dma, dma((CHUNKS,)), dma, dma((CHUNKS,)), dma, dma((CHUNKS,)),
+        dma, dma((CHUNKS,)), dma, dma((CHUNKS,)),
         dma, dma,
     ]
     call = pl.pallas_call(
@@ -499,7 +501,7 @@
         patches, patch_gain[None], patch_bias[None], first_weight, first_bias[None],
         second_weight.T, second_bias[None], image_units, image_owner, image_offset,
         text_states, token_gain[None], expert_ids[0].T, route_weights[0].T,
-        gate_weight, up_weight, down_weight,
+        gate_weight.reshape(2, 4, 512, 128), up_weight.reshape(2, 4, 512, 128), down_weight,
     )
 
 

time: 126 us -> 123 us (0.976)
  the two profiles are of different devices: /device:TPU:34 before, /device:TPU:2 now
where the time goes in v3:
time: 123 us
  Pallas kernels  119 us (97%)
  local copies, waits for them, and re-layouts  4.04 us (3%)
    pallas_call x1, Pallas kernels, body(): call(patches, patch_gain[None], patch_bias[None], first_weight, first_bia...  119 us

profile of v3, /device:TPU:2, one launch (start us, length us, event | category | flops | bytes accessed | tf_op | source)
XLA Modules:
  0.0 123.0 jit_solution(4049065083801106374)
XLA Ops:
  0.0 0.0 copy-start
  0.0 0.0 copy-start.2
  0.0 0.7 copy-done.2
  0.7 0.0 copy-start.1
  0.7 0.6 broadcast_in_dim.17.b1
  1.3 0.0 copy-done
  1.3 0.6 broadcast_in_dim.15.pgain
  1.9 0.0 copy-done.1
  1.9 0.6 broadcast_in_dim.16.pbias
  2.5 119.0 %shard_map.163 = bf16[1,128,512]{2,1,0:T(8,128)(2,1)} custom-call(bf16[1,64,4608]{2,1,0:T(8,128)(2,1)} %patches.1, f32[1,1152]{1,0:T(1,128)} %broadcast_in_dim.15.pgain, f32[1,1152]{1,0:T(1,128)} %broadcast_in_dim.16.pbias, bf16[144,288]{1,0:T(8,128)(2,1)} %w1.1, f32[1,288]{1,0:T(1,128)} %broadcast_in_dim.17.b1, bf16[288,128]{1,0:T(8,128)(2,1)} %bitcast.13, ...), custom_call_target="tpu_custom_call" | custom-call | tf_op jit(solution)/shard_map/pallas_call | solution.py:500
  121.4 1.6 %copy.19 = bf16[1,128,512]{2,1,0:T(8,128)(2,1)} copy(bf16[1,128,512]{2,1,0:T(8,128)(2,1)} %shard_map.163) | data formatting | bytes 262144
Async XLA Ops:
  0.0 1.3 %copy-start = (f32[1152]{0:T(1024)S(1)}, f32[1152]{0:T(1024)}, u32[]{:S(2)}) copy-start(f32[1152]{0:T(1024)} %param.18) | copy-start | bytes 13828
  0.0 0.7 copy-start.2
  0.7 1.2 copy-start.1

commit v4 on v3

--- a/solution.py
+++ b/solution.py
@@ -11,9 +11,12 @@
 MESH = pl.DeviceIdType.MESH
 
 PLANES = 16
-CHUNKS = 4
+CHUNKS = 8
 PER = PLANES // CHUNKS
 ROWS = PER * 32
+PARTS = CHUNKS + 1
+FULL = CHUNKS - 1
+MOVED = PER * FULL
 
 
 DISTANCES = (0, 8, 1, 15, 7, 9, 2, 14, 6, 10, 3, 13, 5, 11, 4, 12)
@@ -44,7 +47,7 @@
     img_s, img_r, tx, wt, pick, st, xs, xr, xk, wgu, dw, gx, ps, pr, ss, act_s, act_r, ob, rb,
     s_w, r_w, s_c, r_c, l_sem, s_gu, r_gu, s_one, r_one, s_info, r_info, s_p2, r_p2,
     s_img, r_img, s_disp, r_disp, s_ag, r_ag, s_rs, r_rs, s_act, r_act,
-    s_ret, r_ret,
+    s_ret, r_ret, s_moved,
 ):
     e = lax.axis_index("expert")
     t = lax.axis_index("tensor")
@@ -71,9 +74,6 @@
     for k, source in enumerate((gate, up)):
         local.append((source.at[:, x], wgu.at[x, :, :, pl.ds(128 * k, 128)]))
     local = [pltpu.make_async_copy(a, b, l_sem.at[i]) for i, (a, b) in enumerate(local)]
-    for copy in local:
-        copy.start()
-
     barrier = pltpu.get_barrier_semaphore()
     after = yh * 16 + lax.rem(z + 1, 16)
     ahead = yh * 16 + lax.rem(z + 15, 16)
@@ -90,6 +90,9 @@
     greet(expert=far)
     greet(expert=far, tensor=across)
 
+    for copy in local:
+        copy.start()
+
     g1[0, :144, :] = w1[:, :256]
     for r in range(9):
         low = 144 if r < 8 else 160
@@ -106,30 +109,34 @@
         for ref, sem in drains:
             wait(ref, sem)
 
-        @pl.when(core == 1)
-        def _():
-            for w, g in enumerate(gathered):
+        for w, g in enumerate(gathered):
+
+            @pl.when(core == 1)
+            def _(w=w, g=g):
                 wait(g.at[pl.ds(1, 15)], s_w.at[w])
                 wait(g.at[pl.ds(1, 15)], s_c.at[w])
 
     gathered = (g1, g2)
-
-    def hand_on(first, count):
-        for w, g in enumerate(gathered):
+    pieces = (((0, 0, 96), (1, 96, 80)), ((2, 0, 288),))
+
+    def ring(w, step):
+        g = gathered[w]
+
+        def hand_on(first, count):
             blocks = g.at[pl.ds(first, count)]
             send(blocks, blocks, s_c.at[w], r_c.at[w], dp=0)
 
-    def ring(step):
-        for w, g in enumerate(gathered):
+        for k, low, size in pieces[w]:
+            rows = pl.ds(low, size)
             for way, to in enumerate((after, ahead)):
                 if step < 8 - way:
                     here, there = (step, step + 1) if way == 0 else ((16 - step) % 16, 15 - step)
                     if step > 0:
-                        wait(g.at[here], r_w.at[w, way, step - 1])
-                    send(g.at[here], g.at[there], s_w.at[w], r_w.at[w, way, step], expert=to)
+                        wait(g.at[here, rows], r_w.at[k, way, step - 1])
+                    send(g.at[here, rows], g.at[there, rows], s_w.at[w], r_w.at[k, way, step], expert=to)
                 elif step == 8 - way:
                     here = step if way == 0 else 16 - step
-                    wait(g.at[here], r_w.at[w, way, step - 1])
+                    wait(g.at[here, rows], r_w.at[k, way, step - 1])
         if step == 3:
             hand_on(1, 3)
             hand_on(13, 3)
@@ -141,7 +148,7 @@
 
     @pl.when(core == 1)
     def _():
-        ring(0)
+        ring(0, 0)
 
     far_half = pl.ds(pl.multiple_of(2304 * (1 - yh), 128), 2304)
     sends.append(
@@ -214,7 +221,7 @@
         v = pv[g, :, part].astype(F32)
         center = v - jnp.mean(v, axis=1, keepdims=True)
         variance = jnp.mean(center * center, axis=1, keepdims=True)
-        scaled = center * lax.rsqrt(variance + 1e-06) * pgain[...] + pbias[...]
+        scaled = center * lax.rsqrt(variance + 1e-06) * pgain[...].reshape(1, 1152) + pbias[...].reshape(1, 1152)
         for o in range(8):
             xz[8 * p + o, g] = scaled[:, 144 * o : 144 * o + 144].astype(BF)
 
@@ -240,7 +247,9 @@
 
         @pl.when(core == 1)
         def _():
-            ring(s + 1)
+            ring(0, s + 1)
+            if s + 1 >= 2:
+                ring(1, s + 1 - 2)
 
         for job in jobs.get(s, ()):
             job()
@@ -262,10 +271,17 @@
     for r in range(8):
         p1s[128:144, 32 * r : 32 * r + 32] = tail[16 * r : 16 * r + 16, :32].astype(BF)
     sends.append(send(p1s, p1r, s_one.at[3], r_one.at[3], expert=far))
-    for d in range(1, 16):
-        send(info_s.at[d], info_r.at[d], s_info, r_info, expert=yh * 16 + lax.rem(z + d, 16))
-    info_r[0] = info_s[0]
-    drains.append((info_r.at[pl.ds(0, 15)], s_info))
+
+    @pl.when(core == 1)
+    def _():
+        ring(1, 7)
+        ring(1, 8)
+
+    def tell(first, last):
+        for d in range(first, last):
+            send(info_s.at[d], info_r.at[d], s_info, r_info, expert=yh * 16 + lax.rem(z + d, 16))
+
+    tell(1, 8)
 
     @pl.when(core == 0)
     def _():
@@ -273,14 +289,16 @@
 
     chosen = swap_own[:128] + swap_far[:128]
 
+    bias = b1[...].reshape(1, 288)
+
     def gelu(v):
         return (0.5 * v * (1.0 + lax.erf(v * (0.5**0.5)))).astype(BF)
 
     wait(p1r, r_one.at[3])
-    hid[:, :256] = gelu(main + p1r[:128].astype(F32) + b1[:, :256])
+    hid[:, :256] = gelu(main + p1r[:128].astype(F32) + bias[:, :256])
     for r in range(8):
         far_tail = p1r[128:144, 32 * r : 32 * r + 32].astype(F32)
-        hid[16 * r : 16 * r + 16, 256:] = gelu(tail[16 * r : 16 * r + 16, :32] + far_tail + b1[:, 256:])
+        hid[16 * r : 16 * r + 16, 256:] = gelu(tail[16 * r : 16 * r + 16, :32] + far_tail + bias[:, 256:])
 
     def second(tt):
         k = 2 * lax.rem(tt, 4) + tt // 4
@@ -292,6 +310,9 @@
         p2s[i - 1] = second(tt).astype(BF)
         send(p2s.at[i - 1], p2r.at[i - 1], s_p2, r_p2, tensor=tt)
     drains.append((p2r.at[pl.ds(0, 7)], s_p2))
+    tell(8, 16)
+    info_r[0] = info_s[0]
+    drains.append((info_r.at[pl.ds(0, 15)], s_info))
     total = second(t) + b2[:, pl.ds(pl.multiple_of(col, 128), 256)]
     wait(p2r.at[pl.ds(0, 7)], r_p2)
     for i in range(7):
@@ -301,7 +322,7 @@
     rows = nn(chosen, emb).reshape(16, 8, 256)
     img_s[...] = jnp.concatenate([rows[:, :, :128], rows[:, :, 128:]], axis=1).astype(BF)
     img_r[0] = img_s[0]
-    for d in range(1, 16):
+    for d in sorted(range(1, 16), key=lambda d: abs(d - 8)):
         send(img_s.at[d], img_r.at[d], s_img, r_img, expert=yh * 16 + lax.rem(z + d, 16))
 
     drains.append((img_r.at[pl.ds(0, 15)], s_img))
@@ -328,10 +349,13 @@
 
     for oy in range(2):
         xs[:, :, 16 * oy : 16 * oy + 16, :] = nn(pick[oy], st[oy]).astype(BF).reshape(16, 2, 16, 256)
-    for p in range(16):
-        if p == HERE:
-            continue
-        send(xs.at[p], xr.at[p], s_disp, r_disp.at[p], expert=yh * 16 + lax.rem(z + DISTANCES[p], 16))
+    for p in range(MOVED):
+        if p != HERE:
+            send(xs.at[p], xr.at[p], s_disp, r_disp.at[p], expert=yh * 16 + lax.rem(z + DISTANCES[p], 16))
+    for p in range(MOVED, 16):
+        place = p + PER * (1 - core)
+        to = yh * 16 + lax.rem(z + DISTANCES[p], 16)
+        send(xs.at[p], xr.at[place], s_disp, r_disp.at[place], expert=to, dp=1)
 
     drains.append((xr.at[pl.ds(0, 15)], s_disp))
 
@@ -401,29 +425,45 @@
         wait(act_r.at[c, :, pl.ds(0, 896)], r_act.at[c])
         ob[PER * c : PER * c + PER] = nn(act_r[c], dw[...]).astype(BF).reshape(PER, 2, 16, 512)
         for p in range(PER * c, PER * c + PER):
-            zz = lax.rem(z - DISTANCES[p] + 16, 16)
-            dst = rb.at[2 * p + yh]
+            home = p - PER if c == CHUNKS else p
+            zz = lax.rem(z - DISTANCES[home] + 16, 16)
+            dst = rb.at[2 * home + yh]
             if p == HERE:
                 rb[2 * p + yh] = ob[p, yh]
                 send(ob.at[p, 1 - yh], dst, s_ret, r_ret, expert=far)
             else:
                 for oy in range(2):
-                    send(ob.at[p, oy], dst, s_ret, r_ret, expert=oy * 16 + zz)
-
-    for turn in range(CHUNKS + 4):
-        if turn < CHUNKS:
-            forward(turn)
-        if 0 <= turn - 1 < CHUNKS:
-            project(turn - 1)
-        if 0 <= turn - 2 < CHUNKS:
-            activate(turn - 2)
-        if 0 <= turn - 3 < CHUNKS:
-            produce(turn - 3)
-
-    drains.append((xk.at[:, pl.ds(0, 3)], s_ag))
-    drains.append((pr, s_rs))
-    drains.append((act_r.at[:, :, pl.ds(0, 896)], s_act))
-    drains.append((rb.at[pl.ds(0, 31)], s_ret))
+                    if c == CHUNKS:
+                        send(ob.at[p, oy], dst, s_moved, r_ret, expert=oy * 16 + zz, dp=0)
+                    else:
+                        send(ob.at[p, oy], dst, s_ret, r_ret, expert=oy * 16 + zz)
+
+    def on_turn(step, c):
+        if 0 <= c < FULL:
+            step(c)
+        elif FULL <= c < PARTS:
+
+            @pl.when(core == 1)
+            def _():
+                step(c)
+
+    for turn in range(PARTS + 3):
+        on_turn(forward, turn)
+        on_turn(project, turn - 1)
+        on_turn(activate, turn - 2)
+        on_turn(produce, turn - 3)
+
+    for count, parts in ((2 * MOVED - 1, FULL), (31, PARTS)):
+
+        @pl.when(core == (1 if parts == PARTS else 0))
+        def _(count=count, parts=parts):
+            wait(xk.at[pl.ds(0, PER * parts), pl.ds(0, 3)], s_ag)
+            wait(pr.at[pl.ds(0, parts)], s_rs)
+            wait(act_r.at[pl.ds(0, parts), :, pl.ds(0, 896)], s_act)
+            wait(rb.at[pl.ds(0, count)], s_ret)
+            if parts == PARTS:
+                wait(ob.at[pl.ds(16, PER)], s_moved)
+
     weight = pick[yh].astype(F32).reshape(32, 16, 128) * wt[...].reshape(32, 1, 128)
     weight = weight.reshape(512, 128)
     high = weight.astype(BF)
@@ -465,24 +505,24 @@
         pltpu.VMEM((2, 512, 128), BF),
         pltpu.VMEM((2, 128, 256), BF),
         pltpu.VMEM((16, 2, 32, 256), BF),
-        pltpu.VMEM((16, 2, 32, 256), BF),
-        pltpu.VMEM((16, 4, 32, 256), BF),
+        pltpu.VMEM((16 + PER, 2, 32, 256), BF),
+        pltpu.VMEM((16 + PER, 4, 32, 256), BF),
         pltpu.VMEM((4, 2, 512, 256), BF),
         pltpu.VMEM((1024, 512), BF),
         pltpu.VMEM((ROWS, 1024), BF),
-        pltpu.VMEM((CHUNKS, 4, ROWS + 16, 256), BF),
-        pltpu.VMEM((CHUNKS, 3, ROWS + 16, 256), BF),
-        pltpu.VMEM((CHUNKS, 8, ROWS), F32),
-        pltpu.VMEM((CHUNKS, ROWS, 128), BF),
-        pltpu.VMEM((CHUNKS, ROWS, 1024), BF),
-        pltpu.VMEM((16, 2, 16, 512), BF),
+        pltpu.VMEM((PARTS, 4, ROWS + 16, 256), BF),
+        pltpu.VMEM((PARTS, 3, ROWS + 16, 256), BF),
+        pltpu.VMEM((PARTS, 8, ROWS), F32),
+        pltpu.VMEM((PARTS, ROWS, 128), BF),
+        pltpu.VMEM((PARTS, ROWS, 1024), BF),
+        pltpu.VMEM((16 + PER, 2, 16, 512), BF),
         pltpu.VMEM((32, 16, 512), BF),
-        dma((2,)), dma((2, 2, 8)), dma((2,)), dma((2,)),
+        dma((2,)), dma((3, 2, 8)), dma((2,)), dma((2,)),
         dma((5,)), dma, dma, dma((4,)), dma((4,)),
         dma, dma, dma, dma, dma, dma,
-        dma, dma((16,)), dma, dma((CHUNKS,)),
-        dma, dma((CHUNKS,)), dma, dma((CHUNKS,)),
-        dma, dma,
+        dma, dma((16 + PER,)), dma, dma((PARTS,)),
+        dma, dma((PARTS,)), dma, dma((PARTS,)),
+        dma, dma, dma,
     ]
     call = pl.pallas_call(
         kernel,
@@ -498,7 +538,7 @@
         ),
     )
     return call(
-        patches, patch_gain[None], patch_bias[None], first_weight, first_bias[None],
+        patches, patch_gain, patch_bias, first_weight, first_bias,
         second_weight.T, second_bias[None], image_units, image_owner, image_offset,
         text_states, token_gain[None], expert_ids[0].T, route_weights[0].T,
         gate_weight.reshape(2, 4, 512, 128), up_weight.reshape(2, 4, 512, 128), down_weight,

time: 123 us -> 119 us (0.967)
  the two profiles are of different devices: /device:TPU:2 before, /device:TPU:32 now
where the time goes in v4:
time: 119 us
  Pallas kernels  117 us (98%)
  local copies, waits for them, and re-layouts  1.57 us (1%)
    pallas_call x1, Pallas kernels, body(): call(patches, patch_gain, patch_bias, first_weight, first_bias, second_we...  117 us

profile of v4, /device:TPU:32, one launch (start us, length us, event | category | flops | bytes accessed | tf_op | source)
XLA Modules:
  0.0 118.9 jit_solution(16451098716775491141)
XLA Ops:
  0.0 117.3 %shard_map.163 = bf16[1,128,512]{2,1,0:T(8,128)(2,1)} custom-call(bf16[1,64,4608]{2,1,0:T(8,128)(2,1)} %patches.1, f32[1152]{0:T(1024)} %pgain.1, f32[1152]{0:T(1024)} %pbias.1, bf16[144,288]{1,0:T(8,128)(2,1)} %w1.1, f32[288]{0:T(512)} %b1.1, bf16[288,128]{1,0:T(8,128)(2,1)} %bitcast.13, f32[1,4096]{1,0:T(1,128)} %bitcast.14, s32[1,32]{1,0:T(1,128)} %units.1, ...), custom_call_target="tpu_custom_call" | custom-call | tf_op jit(solution)/shard_map/pallas_call | solution.py:540
  117.4 1.6 %copy.19 = bf16[1,128,512]{2,1,0:T(8,128)(2,1)} copy(bf16[1,128,512]{2,1,0:T(8,128)(2,1)} %shard_map.163) | data formatting | bytes 262144

commit v5 on v4

--- a/solution.py
+++ b/solution.py
@@ -137,14 +137,14 @@
                 elif step == 8 - way:
                     here = step if way == 0 else 16 - step
                     wait(g.at[here, rows], r_w.at[k, way, step - 1])
-        if step == 3:
-            hand_on(1, 3)
-            hand_on(13, 3)
-        if step == 6:
-            hand_on(4, 3)
-            hand_on(10, 3)
+        if step == 4:
+            hand_on(1, 4)
+            hand_on(12, 4)
+        if step == 7:
+            hand_on(5, 3)
+            hand_on(9, 3)
         if step == 8:
-            hand_on(7, 3)
+            hand_on(8, 1)
 
     @pl.when(core == 1)
     def _():

time: 119 us -> 117 us (0.983)
    pallas_call x1, Pallas kernels: 117 us -> 116 us  [body(): call(patches, patch_gain, patch_bias, first_weight, first_bias, second_we...]
where the time goes in v5:
time: 117 us
  Pallas kernels  116 us (99%)
  local copies, waits for them, and re-layouts  1.57 us (1%)
    pallas_call x1, Pallas kernels, body(): call(patches, patch_gain, patch_bias, first_weight, first_bias, second_we...  116 us

profile of v5, /device:TPU:32, one launch (start us, length us, event | category | flops | bytes accessed | tf_op | source)
XLA Modules:
  0.0 117.3 jit_solution(563127086159361546)
XLA Ops:
  0.0 115.7 %shard_map.163 = bf16[1,128,512]{2,1,0:T(8,128)(2,1)} custom-call(bf16[1,64,4608]{2,1,0:T(8,128)(2,1)} %patches.1, f32[1152]{0:T(1024)} %pgain.1, f32[1152]{0:T(1024)} %pbias.1, bf16[144,288]{1,0:T(8,128)(2,1)} %w1.1, f32[288]{0:T(512)} %b1.1, bf16[288,128]{1,0:T(8,128)(2,1)} %bitcast.13, f32[1,4096]{1,0:T(1,128)} %bitcast.14, s32[1,32]{1,0:T(1,128)} %units.1, ...), custom_call_target="tpu_custom_call" | custom-call | tf_op jit(solution)/shard_map/pallas_call | solution.py:540
  115.7 1.6 %copy.19 = bf16[1,128,512]{2,1,0:T(8,128)(2,1)} copy(bf16[1,128,512]{2,1,0:T(8,128)(2,1)} %shard_map.163) | data formatting | bytes 262144
